TPU v7x, 128 devices: a whole 4x4x4 slice. The times are simulated.
128 devices in a mesh: sample: 16 (over z, x_hi, core), variant: 8 (over y, x_lo).
Axes of the slice: x: 4 (x_hi: 2, x_lo: 2; x = x_hi * 2 + x_lo), y: 4, z: 4, core: 2. Of those that a mesh axis runs over, the one named last changes fastest.
Arguments:
- genotype: bfloat16 [32768, 16384], P('sample', 'variant'), may hold values from 0 to 2
- covariates: float32 [32768, 64], P('sample'), as said below
- outcome: float32 [32768, 256], P('sample', 'variant'), may hold values from 0 to 1
- cohort: int32 [32768], P('sample'), may hold values from 0 to 15
- measured: int32 [256, 16], P('variant'), may hold values from 0 to 1
Outputs:
- z_robust: float32 [256, 16384], P('sample', 'variant')
- z_model: float32 [256, 16384], P('sample', 'variant')
Inputs may be any that keep to these rules, and one draw needn't show every extreme that they name: `covariates`: the first column is all ones.
All inputs are finite; a program needn't handle non-finite values.
Results may differ from a plain program's by a relative error of at most 0.004.
Values may be sent and summed in bfloat16 or wider, within the bound.
A program may use at most 128 MiB of HBM per device.

v0:
```python
import jax
import jax.numpy as jnp
from jax import lax
from jax.sharding import PartitionSpec as P

ITERS = 4


epsilon = 1e-06
highest = lax.Precision.HIGHEST


def chol_solve(matrix, right):
    factor = jnp.linalg.cholesky(matrix)
    middle = jax.scipy.linalg.solve_triangular(factor, right, lower=True)
    return jax.scipy.linalg.solve_triangular(factor, middle, lower=True, trans=1)


def newton_step(hess, grad, width):
    square = hess.reshape(hess.shape[0], width, width)
    return chol_solve(square, grad[..., None])[..., 0]


def per_device(genotype, covariates, outcome, cohort, measured):
    local_rows, width = covariates.shape
    cohort_count = measured.shape[1]
    onehot = (cohort[:, None] == jnp.arange(cohort_count, dtype=jnp.int32)[None, :]).astype(
        jnp.float32
    )
    mask = jnp.dot(onehot, measured.T.astype(jnp.float32), precision=highest)
    outer = (covariates[:, :, None] * covariates[:, None, :]).reshape(local_rows, width * width)
    gram, cross = lax.psum(
        (
            jnp.dot(covariates.T, covariates, precision=highest),
            jnp.dot(covariates.T, genotype.astype(jnp.float32), precision=highest),
        ),
        "sample",
    )
    beta = jnp.zeros((outcome.shape[1], width), jnp.float32)
    for step_index in range(ITERS):
        linear = jnp.dot(covariates, beta.T, precision=highest)
        fitted = jax.nn.sigmoid(linear)
        weights = mask * fitted * (1.0 - fitted)
        working = mask * (outcome - fitted)
        hess_part = jnp.dot(weights.T, outer, precision=highest)
        grad_part = jnp.dot(working.T, covariates, precision=highest)
        hess, grad = (
            lax.psum_scatter(hess_part, "sample", scatter_dimension=0, tiled=True),
            lax.psum_scatter(grad_part, "sample", scatter_dimension=0, tiled=True),
        )
        update = lax.all_gather(newton_step(hess, grad, width), "sample", axis=0, tiled=True)
        beta = beta + update
    linear = jnp.dot(covariates, beta.T, precision=highest)
    fitted = jax.nn.sigmoid(linear)
    resid_local = (mask * (outcome - fitted)).astype(jnp.bfloat16)
    wslab_local = (mask * fitted * (1.0 - fitted)).astype(jnp.bfloat16)
    resid, wslab = (
        lax.all_gather(resid_local, "variant", axis=1, tiled=True),
        lax.all_gather(wslab_local, "variant", axis=1, tiled=True),
    )
    resid_sq = (resid.astype(jnp.float32) ** 2).astype(jnp.bfloat16)
    coef = chol_solve(gram, cross)
    proj = genotype.astype(jnp.float32) - jnp.dot(covariates, coef, precision=highest)
    proj_b = proj.astype(jnp.bfloat16)
    proj_sq = (proj * proj).astype(jnp.bfloat16)
    var_cols = genotype.shape[1]
    share = resid.shape[1] // lax.axis_size("sample")
    score = jnp.einsum("np,nv->pv", resid, proj_b, preferred_element_type=jnp.float32)
    robust = jnp.einsum("np,nv->pv", resid_sq, proj_sq, preferred_element_type=jnp.float32)
    model = jnp.einsum("np,nv->pv", wslab, proj_sq, preferred_element_type=jnp.float32)
    totals = lax.psum(jnp.concatenate([score, robust, model], axis=1), "sample")
    owned = lax.dynamic_slice_in_dim(totals, lax.axis_index("sample") * share, share, 0)
    score = owned[:, :var_cols]
    robust = owned[:, var_cols : 2 * var_cols]
    model = owned[:, 2 * var_cols :]
    return (score * lax.rsqrt(robust + epsilon), score * lax.rsqrt(model + epsilon))


def solution(mesh):
    placed = (
        P("sample", "variant"),
        P("sample", None),
        P("sample", "variant"),
        P("sample"),
        P("variant", None),
    )
    return jax.shard_map(
        per_device,
        mesh=mesh,
        in_specs=placed,
        out_specs=(P("sample", "variant"), P("sample", "variant")),
        check_vma=False,
    )
```

profile of v0, /device:TPU:0, one launch (start us, length us, event | category | flops | bytes accessed | tf_op | source)
XLA Modules:
  0.0 1163.0 jit_solution(8243893889616056096)
XLA Ops:
  7.2 1.5 fusion.22
  8.7 12.3 %broadcast_multiply_fusion = f32[2048,64,64]{0,2,1:T(8,128)} fusion(f32[2048,64]{0,1:T(8,128)} %param.11), kind=kLoop, calls=%fused_computation.2 | loop fusion | flops 8388608 | bytes 34078720 | tf_op jit(solution)/shard_map/mul | solution.py:31
  21.0 1.1 fusion.24
  22.1 34.4 %fusion.50 = f32[32,4096]{1,0:T(8,128)} fusion(f32[2048,4096]{0,1:T(8,128)} %bitcast.202, f32[2048,32]{0,1:T(8,128)S(1)} %fusion.22, f32[2048,32]{0,1:T(8,128)S(1)} %fusion.24), kind=kOutput, calls=%fused_computation.70 | convolution fusion | flops 3221422080 | bytes 34603008 | tf_op jit(solution)/shard_map/dot_general | solution.py:45
  56.6 0.6 dynamic-slice
  57.9 0.5 fusion.47
  58.4 70.8 %all-reduce.1 = f32[32,64]{1,0:T(8,128)S(1)} all-reduce(f32[32,64]{1,0:T(8,128)S(1)} %fusion.47), channel_id=7, replica_groups=mesh['sample'=16,'variant'=8] {'sample'}, use_global_device_ids=true, to_apply=%region_3.5.clone | all-reduce | flops 2048 | bytes 16384
  129.2 68.7 %all-reduce.18.cloned.1.call-done = f32[32,4096]{1,0:T(8,128)} async-done(((f32[32,4096]{1,0:T(8,128)}), f32[32,4096]{1,0:T(8,128)}) %all-reduce.18.cloned.1.call-update) | async-done | bytes 524304
  197.9 0.9 constant_dynamic-slice_fusion.7
  199.1 11.7 %custom-call.29 = f32[2,64,64]{2,1,0:T(8,128)S(1)} custom-call(f32[2,64,64]{2,1,0:T(8,128)S(1)} %fusion.73), custom_call_target="Cholesky" | custom-call | tf_op jit(solution)/shard_map/jit(cholesky)/cholesky | solution.py:14
  211.0 9.8 custom-call.31
  220.9 0.2 convolution_bitcast_fusion.7
  221.1 0.2 convolution_bitcast_fusion.6
  221.3 20.6 %all-gather = f32[32,64,1]{1,2,0:T(1,128)S(1)} all-gather(f32[2,64,1]{1,2,0:T(1,128)S(1)} %convolution_bitcast_fusion.6), channel_id=2, replica_groups=mesh['sample'=16,'variant'=8] {'sample'}, dimensions={0}, use_global_device_ids=true | all-gather | bytes 8704 | tf_op jit(solution)/shard_map/all_gather | solution.py:51
  241.9 0.4 fusion.18
  242.3 34.3 %fusion.43 = f32[32,4096]{1,0:T(8,128)} fusion(f32[2048,4096]{0,1:T(8,128)} %bitcast.203, f32[2048,32]{0,1:T(8,128)S(1)} %fusion.18, f32[2048,32]{0,1:T(8,128)S(1)} %fusion.24), kind=kOutput, calls=%fused_computation.63 | convolution fusion | flops 3221422080 | bytes 34603008 | tf_op jit(solution)/shard_map/dot_general | solution.py:45
  276.7 0.5 fusion.40
  277.3 66.7 %all-reduce.3 = f32[32,64]{1,0:T(8,128)S(1)} all-reduce(f32[32,64]{1,0:T(8,128)S(1)} %fusion.40), channel_id=9, replica_groups=mesh['sample'=16,'variant'=8] {'sample'}, use_global_device_ids=true, to_apply=%region_5.0.clone | all-reduce | flops 2048 | bytes 16384
  344.0 69.3 %all-reduce.20.cloned.1.call-done = f32[32,4096]{1,0:T(8,128)} async-done(((f32[32,4096]{1,0:T(8,128)}), f32[32,4096]{1,0:T(8,128)}) %all-reduce.20.cloned.1.call-update) | async-done | bytes 524304
  413.3 0.9 constant_dynamic-slice_fusion.5
  414.5 11.7 %custom-call.32 = f32[2,64,64]{2,1,0:T(8,128)S(1)} custom-call(f32[2,64,64]{2,1,0:T(8,128)S(1)} %fusion.70), custom_call_target="Cholesky" | custom-call | tf_op jit(solution)/shard_map/jit(cholesky)/cholesky | solution.py:14
  426.4 9.8 custom-call.34
  436.5 0.2 convolution_bitcast_fusion.4
  436.7 20.7 %all-gather.1 = f32[32,64,1]{1,2,0:T(1,128)S(1)} all-gather(f32[2,64,1]{1,2,0:T(1,128)S(1)} %convolution_bitcast_fusion.4), channel_id=3, replica_groups=mesh['sample'=16,'variant'=8] {'sample'}, dimensions={0}, use_global_device_ids=true | all-gather | bytes 8704 | tf_op jit(solution)/shard_map/all_gather | solution.py:51
  457.4 0.4 fusion.14
  457.8 34.3 %fusion.36 = f32[32,4096]{1,0:T(8,128)} fusion(f32[2048,4096]{0,1:T(8,128)} %bitcast.204, f32[2048,32]{0,1:T(8,128)S(1)} %fusion.14, f32[2048,32]{0,1:T(8,128)S(1)} %fusion.24), kind=kOutput, calls=%fused_computation.56 | convolution fusion | flops 3221422080 | bytes 34603008 | tf_op jit(solution)/shard_map/dot_general | solution.py:45
  492.2 7.6 fusion.90
  499.8 0.5 fusion.33
  500.4 66.7 %all-reduce.5 = f32[32,64]{1,0:T(8,128)S(1)} all-reduce(f32[32,64]{1,0:T(8,128)S(1)} %fusion.33), channel_id=11, replica_groups=mesh['sample'=16,'variant'=8] {'sample'}, use_global_device_ids=true, to_apply=%region_7.0.clone | all-reduce | flops 2048 | bytes 16384
  567.1 61.7 %all-reduce.22.cloned.1.call-done = f32[32,4096]{1,0:T(8,128)} async-done(((f32[32,4096]{1,0:T(8,128)}), f32[32,4096]{1,0:T(8,128)}) %all-reduce.22.cloned.1.call-update) | async-done | bytes 524304
  628.8 0.9 constant_dynamic-slice_fusion.3
  629.9 11.7 %custom-call.35 = f32[2,64,64]{2,1,0:T(8,128)S(1)} custom-call(f32[2,64,64]{2,1,0:T(8,128)S(1)} %fusion.67), custom_call_target="Cholesky" | custom-call | tf_op jit(solution)/shard_map/jit(cholesky)/cholesky | solution.py:14
  641.9 9.8 custom-call.37
  651.9 0.2 convolution_bitcast_fusion.2
  652.1 20.9 %all-gather.2 = f32[32,64,1]{1,2,0:T(1,128)S(1)} all-gather(f32[2,64,1]{1,2,0:T(1,128)S(1)} %convolution_bitcast_fusion.2), channel_id=4, replica_groups=mesh['sample'=16,'variant'=8] {'sample'}, dimensions={0}, use_global_device_ids=true | all-gather | bytes 8704 | tf_op jit(solution)/shard_map/all_gather | solution.py:51
  673.0 0.4 fusion.10
  673.4 34.3 %fusion.29 = f32[32,4096]{1,0:T(8,128)} fusion(f32[2048,4096]{0,1:T(8,128)} %bitcast.205, f32[2048,32]{0,1:T(8,128)S(1)} %fusion.10, f32[2048,32]{0,1:T(8,128)S(1)} %fusion.24), kind=kOutput, calls=%fused_computation.49 | convolution fusion | flops 3221422080 | bytes 34603008 | tf_op jit(solution)/shard_map/dot_general | solution.py:45
  707.9 12.3 %copy.58 = bf16[2048,2048]{0,1:T(8,128)(2,1)} copy(bf16[2048,2048]{1,0:T(8,128)(2,1)} %param.10) | data formatting | bytes 16777216 | tf_op args[0]
  720.2 0.6 fusion.89
  720.8 0.5 fusion.26
  721.3 66.9 %all-reduce.8 = (f32[32,64]{1,0:T(8,128)S(1)}, f32[64,64]{0,1:T(8,128)S(1)}) all-reduce(f32[32,64]{1,0:T(8,128)S(1)} %fusion.26, f32[64,64]{0,1:T(8,128)S(1)} %fusion.89), channel_id=13, replica_groups=mesh['sample'=16,'variant'=8] {'sample'}, use_global_device_ids=true, to_apply=%region_9.0.clone | all-reduce | flops 6144 | bytes 49152
  788.3 58.7 %all-reduce.24.cloned.1.call-done = (f32[32,4096]{1,0:T(8,128)}, f32[64,2048]{1,0:T(8,128)}) async-done(((f32[32,4096]{1,0:T(8,128)}, f32[64,2048]{1,0:T(8,128)}), (f32[32,4096]{1,0:T(8,128)}, f32[64,2048]{1,0:T(8,128)})) %all-reduce.24.cloned.1.call-update) | async-done | bytes 1048592
  847.0 0.9 constant_dynamic-slice_fusion.1
  848.1 11.7 %custom-call.38 = f32[2,64,64]{2,1,0:T(8,128)S(1)} custom-call(f32[2,64,64]{2,1,0:T(8,128)S(1)} %fusion.64), custom_call_target="Cholesky" | custom-call | tf_op jit(solution)/shard_map/jit(cholesky)/cholesky | solution.py:14
  860.1 9.8 custom-call.40
  870.1 0.2 convolution_bitcast_fusion
  870.3 20.3 %all-gather.3 = f32[32,64,1]{1,2,0:T(1,128)S(1)} all-gather(f32[2,64,1]{1,2,0:T(1,128)S(1)} %convolution_bitcast_fusion), channel_id=5, replica_groups=mesh['sample'=16,'variant'=8] {'sample'}, dimensions={0}, use_global_device_ids=true | all-gather | bytes 8704 | tf_op jit(solution)/shard_map/all_gather | solution.py:51
  890.6 1.2 multiply_convert_fusion.4
  891.7 0.2 all-gather.9.cloned.1.call-start
  892.0 5.8 cholesky.42
  897.9 0.7 compare_reduce_fusion.4
  898.6 0.7 fusion.74
  899.3 4.9 custom-call.19
  904.2 1.7 fusion.77
  905.9 0.6 fusion.75
  906.5 16.0 %fusion.91 = f32[2048,2048]{1,0:T(8,128)} fusion(f32[64,2048]{1,0:T(8,128)S(1)} %fusion.75, f32[2048,64]{0,1:T(8,128)S(1)} %copy-done), kind=kOutput, calls=%fused_computation.143 | convolution fusion | flops 3221225472 | bytes 17825792 | tf_op jit(solution)/shard_map/dot_general | solution.py:63
  922.5 7.8 all-gather.7.cloned.1.call-done
  930.3 11.1 fusion.23
  941.4 12.0 %fusion.1 = f32[256,2048]{1,0:T(8,128)} fusion(bf16[2048,256]{0,1:T(8,128)(2,1)S(1)} %copy-done.2, f32[2048,2048]{1,0:T(8,128)} %fusion.91, bf16[2048,2048]{0,1:T(8,128)(2,1)} %copy.58), kind=kOutput, calls=%fused_computation.4 | convolution fusion | flops 2160066560 | bytes 28311552 | tf_op jit(solution)/shard_map/np,nv->pv/dot_general | solution.py:68
  953.4 19.0 %all-gather.9.cloned.1.call-done = bf16[2048,256]{0,1:T(8,128)(2,1)} async-done(((bf16[2048,32]{0,1:T(8,128)(2,1)}), bf16[2048,256]{0,1:T(8,128)(2,1)}) %all-gather.9.cloned.1.call-update) | async-done | bytes 1048592 | tf_op jit(solution)/shard_map/all_gather | solution.py:59
  972.5 9.9 fusion.88
  982.4 3.1 pad_maximum_fusion
  985.5 168.7 %all-reduce.16.cloned.1.call-done = f32[256,6144]{1,0:T(8,128)} async-done(((f32[256,6144]{1,0:T(8,128)}), f32[256,6144]{1,0:T(8,128)}) %all-reduce.16.cloned.1.call-update) | async-done | bytes 6291472 | tf_op jit(solution)/shard_map/psum | solution.py:71
  1154.2 1.8 fusion.55
  (65 shorter events, 2.8 us)
Async XLA Ops:
  7.2 190.8 %all-reduce.18.cloned.1.call-start = ((), (), s32[]{:S(2)}) async-start(), calls=%async_computation.3 | async-start | bytes 1048576
  8.7 12.3 %copy-start.4 = (s32[2048]{0:T(1024)S(1)}, s32[2048]{0:T(1024)}, u32[]{:S(2)}) copy-start(s32[2048]{0:T(1024)} %param.13) | copy-start | bytes 24580
  8.7 12.3 %copy-start.5 = (s32[32,16]{0,1:T(8,128)S(1)}, s32[32,16]{0,1:T(8,128)}, u32[]{:S(2)}) copy-start(s32[32,16]{0,1:T(8,128)} %param.14) | copy-start | bytes 6148
  22.1 34.5 %copy-start.6 = (u32[128]{0:T(128)S(1)}, u32[128]{0:T(128)}, u32[]{:S(2)}) copy-start(u32[128]{0:T(128)} %constant.105) | copy-start | bytes 1540
  22.1 35.8 %copy-start = (f32[2048,64]{0,1:T(8,128)S(1)}, f32[2048,64]{0,1:T(8,128)}, u32[]{:S(2)}) copy-start(f32[2048,64]{0,1:T(8,128)} %param.11) | copy-start | bytes 1572868
  22.1 35.8 %copy-start.3 = (f32[2048,32]{0,1:T(8,128)S(1)}, f32[2048,32]{0,1:T(8,128)}, u32[]{:S(2)}) copy-start(f32[2048,32]{0,1:T(8,128)} %param.12) | copy-start | bytes 786436
  56.5 356.8 %all-reduce.20.cloned.1.call-start = ((), (), s32[]{:S(2)}) async-start(), calls=%async_computation.4 | async-start | bytes 1048576
  276.7 352.1 %all-reduce.22.cloned.1.call-start = ((), (), s32[]{:S(2)}) async-start(), calls=%async_computation.5 | async-start | bytes 1048576
  492.1 354.8 %all-reduce.24.cloned.1.call-start = ((), (), s32[]{:S(2)}) async-start(), calls=%async_computation.6 | async-start | bytes 2097152
  707.8 222.5 %all-gather.7.cloned.1.call-start = ((), (), s32[]{:S(2)}) async-start(), calls=%async_computation | async-start | bytes 1179648 | tf_op jit(solution)/shard_map/all_gather | solution.py:58
  891.7 80.7 %all-gather.9.cloned.1.call-start = ((), (), s32[]{:S(2)}) async-start(), calls=%async_computation.1 | async-start | bytes 1179648 | tf_op jit(solution)/shard_map/all_gather | solution.py:59
  922.4 231.8 %all-reduce.16.cloned.1.call-start = ((), (), s32[]{:S(2)}) async-start(), calls=%async_computation.2 | async-start | bytes 12582912 | tf_op jit(solution)/shard_map/psum | solution.py:71
  930.3 11.1 copy-start.2
  972.5 9.9 copy-start.1
Sparse Core Ops, SparseCore 0:
  56.6 141.2 all-reduce.17
  276.8 136.4 all-reduce.19
  492.3 136.5 all-reduce.21
  707.9 139.0 all-reduce.23
  891.9 38.4 all-gather.6
  932.4 40.0 all-gather.8
  985.7 168.5 all-reduce.15
where the time goes:
time: 1170 us; the launch traced here: 1160 us
  waiting for transfers between devices  454 us (39%)
  blocking collectives  354 us (30%)
  matrix products  205 us (18%)
  other arithmetic  117 us (10%)
  local copies, waits for them, and re-layouts  17.5 us (1%)
  between operations  15.3 us (1%)
    unnamed x4, blocking collectives  271 us
    unnamed x11, waiting for transfers between devices  258 us
    psum x1, waiting for transfers between devices, per_device(): totals = lax.psum(jnp.concatenate([score, robust, model], axis=1), 'sample')  169 us
    dot_general x4, matrix products, per_device(): hess_part = jnp.dot(weights.T, outer, precision=highest)  137 us
    all_gather x4, blocking collectives, per_device(): lax.all_gather(newton_step(hess, grad, width), 'sample', axis=0, tiled=True)  82.5 us
    another operation x16, other arithmetic, chol_solve(): factor = jnp.linalg.cholesky(matrix)  54.1 us
    another operation x11, other arithmetic, chol_solve(): jax.scipy.linalg.solve_triangular(factor, middle, lower=True, trans=1)  45.3 us
  transfers between devices with their start and end apart: 7, of which 7 were waited for; matrix products, arithmetic and copies ran while one was open for 7% of the time, Pallas kernels for 0%

commit v1 on v0

v1 whole, which is shorter than its diff:
```python
import functools

import jax
import jax.numpy as jnp
from jax import lax
from jax.experimental import pallas as pl
from jax.experimental.pallas import tpu as pltpu
from jax.sharding import PartitionSpec as P

ITERS = 4
EPS = 1e-06
HIGHEST = lax.Precision.HIGHEST
F32 = jnp.float32
BF16 = jnp.bfloat16
TILES = 4
PROJ = 256
ROWS = 512


def dot(a, b):
    return jnp.dot(a, b, preferred_element_type=F32)


def exact(a, b):
    return jnp.dot(a, b, preferred_element_type=F32, precision=HIGHEST)


def two(x):
    hi = x.astype(BF16)
    return hi, (x - hi.astype(F32)).astype(BF16)


def fold(x):
    return x + pltpu.roll(x, 64, 1)


def eta_of(rows, xt2):
    low = lax.broadcasted_iota(jnp.int32, rows.shape, 1) < 64
    zero = jnp.zeros_like(rows)
    beta = jnp.concatenate([jnp.where(low, rows, zero), jnp.where(low, zero, rows)], axis=0)
    return exact(beta, xt2)


def sweep(m, g):
    lane = lax.broadcasted_iota(jnp.int32, (1, 128), 1)
    low = lane < 64
    grow = lax.broadcasted_iota(jnp.int32, (64, 1), 0)
    for k in range(64):
        if k % 8 == 0 and k:
            m = m[8:, :]
        r = k % 8
        at = (lane == k) | (lane == k + 64)
        col = jnp.where(low, m[:, k : k + 1], m[:, 64 + k : 65 + k])
        inv = 1.0 / col[r : r + 1, :]
        row = jnp.where(at, -1.0, m[r : r + 1, :]) * inv
        m = jnp.where(at, 0.0, m) - col * row
        if g is not None:
            gcol = jnp.broadcast_to(g[:, k : k + 1], g.shape)
            ginv = 1.0 / gcol[k : k + 1, :]
            gline = jnp.where(at, -1.0, g[k : k + 1, :]) * ginv
            here = grow == k
            g = jnp.where(at | here, 0.0, g) - jnp.where(here, -1.0, gcol) * gline
    return m[8:9, :], g


def kernel(
    ns,
    nv,
    g_hbm,
    xt2_ref,
    x4_ref,
    y_ref,
    zr_ref,
    zm_ref,
    gbuf,
    psq,
    xhl,
    yall,
    wbuf,
    rsp,
    lhs,
    hs,
    hr,
    crs,
    crr,
    grs,
    grr,
    ginv_ref,
    bcur,
    br,
    ball,
    c4,
    cfall,
    r1,
    r2,
    so,
    asd,
    arv,
    bsd,
    brv,
    fin,
    g_sem,
    h_ss,
    h_rs,
    c_ss,
    c_rs,
    gr_ss,
    gr_rs,
    b_ss,
    b_rs,
    f_ss,
    f_rs,
    y_ss,
    y_rs,
    v_ss,
    v_rs,
    a_ss,
    a_rs,
    q_ss,
    q_rs,
):
    s = lax.axis_index("sample")
    v = lax.axis_index("variant")
    core = lax.rem(s, 2)
    myq = s // 2
    low = lax.broadcasted_iota(jnp.int32, (1, 128), 1) < 64

    gcopy = pltpu.make_async_copy(g_hbm, gbuf, g_sem)
    gcopy.start()

    def speer(d):
        return lax.rem(s + d, ns)

    def vpeer(d):
        return lax.rem(v + d, nv)

    def remote(src, dst, ss, rs, sample, variant):
        return pltpu.make_async_remote_copy(
            src_ref=src,
            dst_ref=dst,
            send_sem=ss,
            recv_sem=rs,
            device_id=(sample, variant),
            device_id_type=pl.DeviceIdType.MESH,
        )

    barrier = pltpu.get_barrier_semaphore()

    @pl.loop(1, ns)
    def _(d):
        pl.semaphore_signal(
            barrier, inc=1, device_id=(speer(d), v), device_id_type=pl.DeviceIdType.MESH
        )

    @pl.loop(1, nv)
    def _(d):
        pl.semaphore_signal(
            barrier, inc=1, device_id=(s, vpeer(d)), device_id_type=pl.DeviceIdType.MESH
        )

    hi, lo = two(xt2_ref[0:64, :])
    xhl[0:64, :] = hi
    xhl[64:128, :] = lo
    bcur[...] = jnp.zeros_like(bcur)
    br[...] = jnp.zeros_like(br)
    hs[...] = jnp.zeros_like(hs)
    grams = dot(xhl[...], x4_ref[:, 0:128])
    grs[...] = fold(grams[0:64, :] + grams[64:128, :])

    pl.semaphore_wait(barrier, ns + nv - 2)

    def y_copy(j):
        return remote(y_ref, yall.at[v], y_ss.at[j], y_rs.at[v], s, j)

    def y_from(j):
        return remote(y_ref, yall.at[j], y_ss.at[j], y_rs.at[j], s, j)

    def gr_copy(j):
        return remote(grs, grr.at[s], gr_ss.at[j], gr_rs.at[s], j, v)

    def gr_from(j):
        return remote(grs, grr.at[j], gr_ss.at[j], gr_rs.at[j], j, v)

    def h_copy(j):
        return remote(hs.at[j], hr.at[s], h_ss.at[j], h_rs.at[s], j, v)

    def h_from(j):
        return remote(hs.at[j], hr.at[j], h_ss.at[j], h_rs.at[j], j, v)

    def c_copy(j):
        return remote(crs.at[j], crr.at[s], c_ss.at[j], c_rs.at[s], j, v)

    def c_from(j):
        return remote(crs.at[j], crr.at[j], c_ss.at[j], c_rs.at[j], j, v)

    def b_copy(j):
        return remote(br.at[s], br.at[s], b_ss.at[j], b_rs.at[s], j, v)

    def b_from(j):
        return remote(br.at[s], br.at[j], b_ss.at[j], b_rs.at[j], j, v)

    def f_copy(j):
        return remote(cfall.at[s], cfall.at[s], f_ss.at[j], f_rs.at[s], j, v)

    def f_from(j):
        return remote(cfall.at[s], cfall.at[j], f_ss.at[j], f_rs.at[j], j, v)

    def v_copy(j):
        return remote(ball.at[v], ball.at[v], v_ss.at[j], v_rs.at[v], s, j)

    def v_from(j):
        return remote(ball.at[v], ball.at[j], v_ss.at[j], v_rs.at[j], s, j)

    def each(n, peer, do):
        @pl.loop(1, n)
        def _(d):
            do(peer(d))

    each(ns, speer, lambda j: gr_copy(j).start())
    each(nv, vpeer, lambda j: y_copy(j).start())

    def hessians():
        eta = eta_of(br[:, 0, :], xt2_ref[...])
        fitted = 1.0 / (1.0 + jnp.exp(-eta))
        coded = y_ref[...]
        seen = coded >= 0.0
        wbuf[...] = jnp.where(seen, fitted * (1.0 - fitted), 0.0)
        work = jnp.where(seen, coded - fitted, 0.0)
        r_hi = work.astype(BF16)
        rest = work - r_hi.astype(F32)
        r_mid, r_lo = two(rest)
        rsp[0:32, :] = r_hi
        rsp[32:64, :] = r_mid
        rsp[64:96, :] = r_lo
        gsum = dot(rsp[...], x4_ref[:, 0:128])
        gsum = fold(gsum[0:32] + gsum[32:64] + gsum[64:96])
        gpair = jnp.where(low, gsum[0:16], gsum[16:32])
        for j in range(16):
            hs[j, 64:65, :] = gpair[j : j + 1]

        @pl.loop(0, 4)
        def _(group):
            @pl.loop(0, 4)
            def _(i):
                for half in range(2):
                    w = wbuf[pl.ds(group * 4 + i + 16 * half, 1), :]
                    base = pl.multiple_of(i * 256 + half * 128, 128)
                    for c in range(4):
                        cols = slice(c * 512, (c + 1) * 512)
                        hi, lo = two(xt2_ref[0:64, cols] * w[:, cols])
                        lhs[pl.ds(base, 64), cols] = hi
                        lhs[pl.ds(base + 64, 64), cols] = lo

            out = dot(lhs[...], x4_ref[:, 0:128])
            for i in range(4):
                part = out[i * 256 : (i + 1) * 256]
                first = fold(part[0:64] + part[64:128])
                second = fold(part[128:192] + part[192:256])
                hs[group * 4 + i, 0:64, :] = jnp.where(low, first, second)

    def crosses():
        @pl.loop(0, 8)
        def _(t):
            out = dot(xhl[...], gbuf[:, pl.ds(pl.multiple_of(t * 256, 256), 256)])
            out = out[0:64] + out[64:128]
            crs[2 * t] = out[:, 0:128]
            crs[2 * t + 1] = out[:, 128:256]

    def project(t):
        for h in range(2):
            part = cfall[2 * t + h]
            cols = slice(h * 128, (h + 1) * 128)
            c4[0:64, cols] = part[0:64]
            c4[64:128, cols] = part[0:64]
            c4[128:192, cols] = part[64:128]
            c4[192:256, cols] = part[64:128]
        cols = pl.ds(pl.multiple_of(t * PROJ, PROJ), PROJ)

        @pl.loop(0, 2048 // ROWS)
        def _(i):
            rows = pl.ds(pl.multiple_of(i * ROWS, ROWS), ROWS)
            proj = gbuf[rows, cols].astype(F32) - dot(x4_ref[rows, :], c4[...])
            gbuf[rows, cols] = proj.astype(BF16)
            psq[rows, cols] = (proj * proj).astype(BF16)

    @pl.loop(0, ITERS)
    def _(it):
        hessians()
        each(ns, speer, lambda j: h_copy(j).start())

        @pl.when(it == 0)
        def _():
            gcopy.wait()
            crosses()
            each(ns, speer, lambda j: c_copy(j).start())
            each(ns, speer, lambda j: gr_from(j).wait_recv())
            grr[s] = grs[...]
            total = grr[0]
            for j in range(1, ns):
                total = total + grr[j]
            ginv_ref[...] = total

        @pl.when(it == 1)
        def _():
            each(ns, speer, lambda j: f_from(j).wait_recv())

        @pl.when(it >= 1)
        def _():
            @pl.loop((it - 1) * 3, jnp.minimum(it * 3, 2048 // PROJ))
            def _(t):
                project(t)

        each(ns, speer, lambda j: h_from(j).wait_recv())
        hr[s] = hs[s]
        total = hr[0]
        for j in range(1, ns):
            total = total + hr[j]
        delta, ginv = sweep(total, ginv_ref[...])
        bcur[0:1, :] = bcur[0:1, :] + delta

        @pl.when(it > 0)
        def _():
            each(ns, speer, lambda j: b_copy(j).wait_send())

        br[s] = bcur[...]
        each(ns, speer, lambda j: b_copy(j).start())

        @pl.when(it == 0)
        def _():
            each(ns, speer, lambda j: c_from(j).wait_recv())
            crr[s] = crs[s]
            cross = crr[0]
            for j in range(1, ns):
                cross = cross + crr[j]
            hi, lo = two(exact(-ginv[:, 0:64], cross))
            cfall[s, 0:64, :] = hi
            cfall[s, 64:128, :] = lo
            each(ns, speer, lambda j: f_copy(j).start())

        each(ns, speer, lambda j: h_copy(j).wait_send())
        each(ns, speer, lambda j: b_from(j).wait_recv())

    each(ns, speer, lambda j: b_copy(j).wait_send())
    ball[v] = br[:, 0, :]
    each(nv, vpeer, lambda j: v_copy(j).start())
    each(nv, vpeer, lambda j: y_from(j).wait_recv())
    yall[v] = y_ref[...]
    each(nv, vpeer, lambda j: v_from(j).wait_recv())

    @pl.loop(0, nv)
    def _(u):
        eta = eta_of(ball[u], xt2_ref[...])
        fitted = 1.0 / (1.0 + jnp.exp(-eta))
        coded = yall[u]
        seen = coded >= 0.0
        resid = jnp.where(seen, coded - fitted, 0.0).astype(BF16)
        wslab = jnp.where(seen, fitted * (1.0 - fitted), 0.0).astype(BF16)
        wide = resid.astype(F32)
        square = (wide * wide).astype(BF16)
        for h in range(2):
            half = slice(h * 16, (h + 1) * 16)
            at = pl.multiple_of(u * 16 + h * 128, 16)
            r1[pl.ds(at, 16), :] = resid[half]
            r2[pl.ds(at, 16), :] = square[half]
            r2[pl.ds(at + 256, 16), :] = wslab[half]

    width = 2048 // TILES

    def a_copy(t):
        return remote(asd.at[t], arv.at[t], a_ss.at[t], a_rs.at[t], s + 1 - 2 * core, v)

    def q_copy(t, q):
        return remote(bsd.at[t, q], brv.at[t, myq], q_ss.at[t, q], q_rs.at[t, myq], 2 * q + core, v)

    def q_from(t, q):
        return remote(bsd.at[t, q], brv.at[t, q], q_ss.at[t, q], q_rs.at[t, q], 2 * q + core, v)

    def others(do):
        @pl.loop(1, ns // 2)
        def _(d):
            do(lax.rem(myq + d, ns // 2))

    @pl.loop(0, TILES + 1)
    def _(t):
        @pl.when(t < TILES)
        def _():
            slot = lax.rem(t, 2)
            cols = pl.ds(pl.multiple_of(t * width, width), width)
            so[slot, 0:256, :] = dot(r1[...], gbuf[:, cols])
            so[slot, 256:768, :] = dot(r2[...], psq[:, cols])

            @pl.loop(0, ns // 2)
            def _(q):
                at = pl.multiple_of((1 - core) * 128 + q * 16, 16)
                hi, lo = two(so[slot, pl.ds(at, 16), :])
                asd[t, q, 0:16, :] = hi
                asd[t, q, 16:32, :] = lo
                asd[t, q, 32:48, :] = so[slot, pl.ds(at + 256, 16), :].astype(BF16)
                asd[t, q, 48:64, :] = so[slot, pl.ds(at + 512, 16), :].astype(BF16)

            a_copy(t).start()

        @pl.when(t > 0)
        def _():
            b = t - 1
            slot = lax.rem(b, 2)
            a_copy(b).wait_recv()

            def total(q):
                at = pl.multiple_of(core * 128 + q * 16, 16)
                score = so[slot, pl.ds(at, 16), :]
                score = score + arv[b, q, 0:16, :].astype(F32) + arv[b, q, 16:32, :].astype(F32)
                robust = so[slot, pl.ds(at + 256, 16), :] + arv[b, q, 32:48, :].astype(F32)
                model = so[slot, pl.ds(at + 512, 16), :] + arv[b, q, 48:64, :].astype(F32)
                return score, robust, model

            def send(q):
                score, robust, model = total(q)
                hi, lo = two(score)
                bsd[b, q, 0:16, :] = hi
                bsd[b, q, 16:32, :] = lo
                bsd[b, q, 32:48, :] = robust.astype(BF16)
                bsd[b, q, 48:64, :] = model.astype(BF16)
                q_copy(b, q).start()

            others(send)
            score, robust, model = total(myq)
            fin[b, 0:16, :] = score
            fin[b, 16:32, :] = robust
            fin[b, 32:48, :] = model

    for t in range(TILES):
        others(lambda q: q_from(t, q).wait_recv())
        brv[t, myq] = jnp.zeros((64, width), BF16)
        score, robust, model = fin[t, 0:16, :], fin[t, 16:32, :], fin[t, 32:48, :]
        for q in range(ns // 2):
            score = score + brv[t, q, 0:16, :].astype(F32) + brv[t, q, 16:32, :].astype(F32)
            robust = robust + brv[t, q, 32:48, :].astype(F32)
            model = model + brv[t, q, 48:64, :].astype(F32)
        cols = slice(t * width, (t + 1) * width)
        zr_ref[:, cols] = score * lax.rsqrt(robust + EPS)
        zm_ref[:, cols] = score * lax.rsqrt(model + EPS)

    each(ns, speer, lambda j: gr_copy(j).wait_send())
    each(ns, speer, lambda j: c_copy(j).wait_send())
    each(ns, speer, lambda j: f_copy(j).wait_send())
    each(nv, vpeer, lambda j: y_copy(j).wait_send())
    each(nv, vpeer, lambda j: v_copy(j).wait_send())

    @pl.loop(0, TILES)
    def _(t):
        a_copy(t).wait_send()
        others(lambda q: q_copy(t, q).wait_send())


def per_device(ns, nv, genotype, covariates, outcome, cohort, measured):
    rows = covariates.shape[0]
    cohorts = measured.shape[1]
    onehot = (jnp.arange(cohorts, dtype=jnp.int32)[:, None] == cohort[None, :]).astype(BF16)
    mask = jnp.dot(measured.astype(BF16), onehot, preferred_element_type=F32)
    coded = jnp.where(mask > 0.5, outcome.T, -1.0)
    xt = covariates.T
    xt2 = jnp.concatenate([xt, xt], axis=0)
    xh = lax.reduce_precision(covariates, 8, 7)
    xl = covariates - xh
    x4 = jnp.concatenate([xh, xl, xh, xl], axis=1).astype(BF16)
    out = jax.ShapeDtypeStruct((256 // ns, 2048), F32)
    vm = pltpu.VMEM
    dma = pltpu.SemaphoreType.DMA
    width = 2048 // TILES
    scratch = [
        vm((2048, 2048), BF16),
        vm((2048, 2048), BF16),
        vm((128, 2048), BF16),
        vm((nv, 32, 2048), F32),
        vm((32, 2048), F32),
        vm((96, 2048), BF16),
        vm((1024, 2048), BF16),
        vm((ns, 72, 128), F32),
        vm((ns, 72, 128), F32),
        vm((ns, 64, 128), F32),
        vm((ns, 64, 128), F32),
        vm((64, 128), F32),
        vm((ns, 64, 128), F32),
        vm((64, 128), F32),
        vm((8, 128), F32),
        vm((ns, 8, 128), F32),
        vm((nv, 16, 128), F32),
        vm((256, PROJ), BF16),
        vm((ns, 128, 128), BF16),
        vm((256, 2048), BF16),
        vm((512, 2048), BF16),
        vm((2, 768, width), F32),
        vm((TILES, ns // 2, 64, width), BF16),
        vm((TILES, ns // 2, 64, width), BF16),
        vm((TILES, ns // 2, 64, width), BF16),
        vm((TILES, ns // 2, 64, width), BF16),
        vm((TILES, 48, width), F32),
        dma,
    ]
    scratch += [dma((ns,))] * 10 + [dma((nv,))] * 4 + [dma((TILES,))] * 2
    scratch += [dma((TILES, ns // 2))] * 2
    return pl.pallas_call(
        functools.partial(kernel, ns, nv),
        out_shape=(out, out),
        in_specs=[pl.BlockSpec(memory_space=pl.ANY)] + [pl.BlockSpec(memory_space=pltpu.VMEM)] * 3,
        out_specs=(pl.BlockSpec(memory_space=pltpu.VMEM),) * 2,
        scratch_shapes=scratch,
        compiler_params=pltpu.CompilerParams(
            collective_id=0, has_side_effects=True, vmem_limit_bytes=60 * 2**20
        ),
        name="score_tests",
    )(genotype, xt2, x4, coded)


def solution(mesh):
    placed = (
        P("sample", "variant"),
        P("sample", None),
        P("sample", "variant"),
        P("sample"),
        P("variant", None),
    )
    return jax.shard_map(
        functools.partial(per_device, mesh.shape["sample"], mesh.shape["variant"]),
        mesh=mesh,
        in_specs=placed,
        out_specs=(P("sample", "variant"), P("sample", "variant")),
        check_vma=False,
    )
```

time: 1170 us -> 201 us (0.17)
  waiting for transfers between devices: 454 us -> 0 us
  blocking collectives: 354 us -> 0 us
  matrix products: 205 us -> 0.93 us
  Pallas kernels: 0 us -> 191 us
  other arithmetic: 117 us -> 4.08 us
  between operations: 15.3 us -> 0.71 us
  local copies, waits for them, and re-layouts: 17.5 us -> 3.82 us
    unnamed x4 -> x0, blocking collectives: 271 us -> none
    unnamed x11 -> x0, waiting for transfers between devices: 258 us -> none
    dot_general x20 -> x1, matrix products: 202 us -> 0.93 us  [per_device(): mask = jnp.dot(measured.astype(BF16), onehot, preferred_element_type=F32)]
    pallas_call x0 -> x1, Pallas kernels: none -> 191 us  [per_device(): pl.pallas_call(functools.partial(kernel, ns, nv), out_shape=(out, out), i...]
    psum x1 -> x0, waiting for transfers between devices: 169 us -> none  [per_device(): totals = lax.psum(jnp.concatenate([score, robust, model], axis=1), 'sample')]
    another operation x27 -> x1, other arithmetic: 99.4 us -> 0.14 us  [the longest x16 54.1 us: chol_solve(): factor = jnp.linalg.cholesky(matrix)]
    all_gather x4 -> x0, blocking collectives: 82.5 us -> none  [per_device(): lax.all_gather(newton_step(hess, grad, width), 'sample', axis=0, tiled=True)]
    all_gather x2 -> x0, waiting for transfers between devices: 26.9 us -> none  [the longest x1 19 us: per_device(): lax.all_gather(wslab_local, 'variant', axis=1, tiled=True)]
  transfers between devices with their start and end apart: 7 -> 0, of which waited for: 7 -> 0; matrix products, arithmetic and copies ran while one was open for 7% -> 0% of each run, Pallas kernels for 0% -> 0%
where the time goes in v1:
time: 201 us
  Pallas kernels  191 us (95%)
  other arithmetic  4.08 us (2%)
  local copies, waits for them, and re-layouts  3.82 us (2%)
    pallas_call x1, Pallas kernels, per_device(): pl.pallas_call(functools.partial(kernel, ns, nv), out_shape=(out, out), i...  191 us

profile of v1, /device:TPU:0, one launch (start us, length us, event | category | flops | bytes accessed | tf_op | source)
XLA Modules:
  0.0 200.8 jit_solution(5658296399056100393)
XLA Ops:
  0.6 0.0 copy-start
  0.6 1.1 reduce_precision.3
  1.8 0.3 copy.9
  2.1 0.0 copy-done
  2.1 0.3 copy.10
  2.5 0.1 fusion.4
  2.6 0.0 copy-start.1
  2.6 0.0 copy-start.2
  2.6 0.0 copy-start.3
  2.7 1.7 pad_maximum_fusion.1.x4_ref
  4.4 1.1 pad_maximum_fusion.xt2_ref
  5.5 0.0 copy-done.1
  5.5 0.0 copy-done.2
  5.5 0.0 copy-done.3
  5.5 0.9 fusion.1.y_ref
  6.4 191.2 %score_tests.1 = (f32[16,2048]{1,0:T(8,128)}, f32[16,2048]{1,0:T(8,128)}) custom-call(bf16[2048,2048]{1,0:T(8,128)(2,1)} %g_hbm.1, f32[128,2048]{1,0:T(8,128)} %pad_maximum_fusion.xt2_ref, bf16[2048,256]{1,0:T(8,128)(2,1)} %pad_maximum_fusion.1.x4_ref, f32[32,2048]{1,0:T(8,128)} %fusion.1.y_ref), custom_call_target="tpu_custom_call" | custom-call | tf_op jit(solution)/shard_map/score_tests/pallas_call | solution.py:503
  197.6 1.6 copy.14
  199.2 1.6 copy.15
Async XLA Ops:
  0.6 1.5 copy-start
  2.6 2.8 %copy-start.1 = (f32[2048,32]{0,1:T(8,128)S(1)}, f32[2048,32]{0,1:T(8,128)}, u32[]{:S(2)}) copy-start(f32[2048,32]{0,1:T(8,128)} %param.7) | copy-start | bytes 786436
  2.6 2.8 %copy-start.2 = (s32[2048]{0:T(1024)S(1)}, s32[2048]{0:T(1024)}, u32[]{:S(2)}) copy-start(s32[2048]{0:T(1024)} %param.8) | copy-start | bytes 24580
  2.6 2.8 %copy-start.3 = (s32[32,16]{0,1:T(8,128)S(1)}, s32[32,16]{0,1:T(8,128)}, u32[]{:S(2)}) copy-start(s32[32,16]{0,1:T(8,128)} %param.9) | copy-start | bytes 6148

commit v2 on v1

v2 whole, which is shorter than its diff:
```python
import functools

import jax
import jax.numpy as jnp
from jax import lax
from jax.experimental import pallas as pl
from jax.experimental.pallas import tpu as pltpu
from jax.sharding import PartitionSpec as P

ITERS = 4
EPS = 1e-06
HIGHEST = lax.Precision.HIGHEST
F32 = jnp.float32
BF16 = jnp.bfloat16
TILES = 4
PROJ = 256
ROWS = 512


def dot(a, b):
    return jnp.dot(a, b, preferred_element_type=F32)


def exact(a, b):
    return jnp.dot(a, b, preferred_element_type=F32, precision=HIGHEST)


def two(x):
    hi = x.astype(BF16)
    return hi, (x - hi.astype(F32)).astype(BF16)


def fold(x):
    return x + pltpu.roll(x, 64, 1)


def exact_t(a, b):
    return lax.dot_general(a, b, (((1,), (1,)), ((), ())), preferred_element_type=F32)


def product(x, y):
    out = []
    for i in range(len(x)):
        line = []
        for j in range(len(y[0])):
            term = x[i][0] * y[0][j]
            for k in range(1, len(y)):
                term = term + x[i][k] * y[k][j]
            line.append(term)
        out.append(line)
    return out


def inverse2(a):
    (p, q), (_, d) = a
    i = 1.0 / (p * d - q * q)
    return [[d * i, -(q * i)], [-(q * i), p * i]]


def inverse4(a):
    right = [r[2:] for r in a[:2]]
    corner = [r[2:] for r in a[2:]]
    flip = lambda x: [list(c) for c in zip(*x)]
    first = inverse2([r[:2] for r in a[:2]])
    lead = product(first, right)
    inner = product(flip(right), lead)
    last = inverse2([[corner[i][j] - inner[i][j] for j in range(2)] for i in range(2)])
    side = product(lead, last)
    more = product(side, flip(lead))
    top = [[first[i][j] + more[i][j] for j in range(2)] + [-side[i][j] for j in range(2)] for i in range(2)]
    return top + [[-side[j][i] for j in range(2)] + last[i] for i in range(2)]


def sweep(m, full):
    lane = lax.broadcasted_iota(jnp.int32, (1, 128), 1)
    low = lane < 64
    place = jnp.where(low, lane, lane - 64)
    height = lax.broadcasted_iota(jnp.int32, (64, 1), 0)
    for k in range(0, 64, 4):
        if not full and k % 8 == 0 and k:
            m = m[8:, :]
        r = k if full else k % 8
        cols = [jnp.where(low, m[:, k + j : k + j + 1], m[:, 64 + k + j : 65 + k + j]) for j in range(4)]
        pivot = [[cols[max(i, j)][r + min(i, j) : r + min(i, j) + 1, :] for j in range(4)] for i in range(4)]
        here = (place >= k) & (place < k + 4)
        lines = [
            [jnp.where(here, jnp.where(place == k + j, -1.0, 0.0), m[r + j : r + j + 1, :])] for j in range(4)
        ]
        lines = product(inverse4(pivot), lines)
        m = jnp.where(here, 0.0, m)
        if full:
            mine = (height >= k) & (height < k + 4)
            m = jnp.where(mine, 0.0, m)
            cols = [jnp.where(mine, jnp.where(height == k + j, -1.0, 0.0), cols[j]) for j in range(4)]
        m = m - product([cols], lines)[0][0]
    return m if full else m[8:9, :]


def kernel(
    ns,
    nv,
    g_hbm,
    xt_ref,
    out_ref,
    cohort_ref,
    meas_ref,
    tot_ref,
    gbuf,
    psq,
    xt4,
    xhl,
    x4,
    ybuf,
    y4,
    yall,
    wbuf,
    lhs,
    hacc,
    hs,
    hr,
    crs,
    crr,
    grs,
    grr,
    ginv_ref,
    bcur,
    br,
    bet,
    ball,
    c4,
    cfall,
    r1,
    r2,
    so,
    asd,
    arv,
    bsd,
    brv,
    fin,
    g_sem,
    c_ss,
    c_rs,
    f_ss,
    f_rs,
    h_ss,
    h_rs,
    gr_ss,
    gr_rs,
    b_ss,
    b_rs,
    x_ss,
    x_rs,
    p_ss,
    p_rs,
    y_ss,
    y_rs,
    v_ss,
    v_rs,
    a_ss,
    a_rs,
    q_ss,
    q_rs,
):
    nz = ns // 4
    s = lax.axis_index("sample")
    v = lax.axis_index("variant")
    z = s // 4
    sub = lax.rem(s, 4)
    core = lax.rem(s, 2)
    xh = sub // 2
    myq = s // 2
    sibling = s + 1 - 2 * core
    across = s + 2 - 4 * xh
    near = v + 1 - 2 * lax.rem(v, 2)
    low = lax.broadcasted_iota(jnp.int32, (1, 128), 1) < 64
    mesh_id = pl.DeviceIdType.MESH

    gcopy = pltpu.make_async_copy(g_hbm, gbuf, g_sem)
    gcopy.start()

    def block(b):
        return pl.ds(pl.multiple_of(b * 2048, 2048), 2048)

    def split(b):
        hi, lo = two(xt4[:, block(b)])
        xhl[0:64, block(b)] = hi
        xhl[64:128, block(b)] = lo

    def block_at(i):
        return 2 * lax.rem(xh + i // 2, 2) + lax.rem(core + i, 2)

    def speer(d):
        return lax.rem(s + d, ns)

    def zpeer(d):
        return lax.rem(z + d, nz)

    def vpeer(d):
        return lax.rem(v + d, nv)

    def remote(src, dst, ss, rs, sample, variant):
        return pltpu.make_async_remote_copy(
            src_ref=src,
            dst_ref=dst,
            send_sem=ss,
            recv_sem=rs,
            device_id=(sample, variant),
            device_id_type=mesh_id,
        )

    def each(n, peer, do):
        @pl.loop(1, n)
        def _(d):
            do(peer(d))

    barrier = pltpu.get_barrier_semaphore()

    def greet(sample, variant):
        pl.semaphore_signal(barrier, inc=1, device_id=(sample, variant), device_id_type=mesh_id)

    plane = 4 * nv
    place = v * 4 + sub

    def ppeer(d):
        return lax.rem(place + d, plane)

    @pl.loop(1, nz)
    def _(d):
        for k in range(4):
            greet(4 * zpeer(d) + k, v)

    each(plane, ppeer, lambda j: greet(4 * z + lax.rem(j, 4), j // 4))

    hot = lax.broadcasted_iota(jnp.int32, (16, 2048), 0) == cohort_ref[...]
    mask = lax.dot_general(
        meas_ref[...].astype(BF16),
        hot.astype(BF16),
        (((0,), (0,)), ((), ())),
        preferred_element_type=F32,
    )
    ybuf[...] = jnp.where(mask > 0.5, out_ref[...], -1.0)
    own = block(sub)
    y4[:, own] = ybuf[pl.ds(pl.multiple_of(sub * 8, 8), 8), :]
    xt4[:, own] = xt_ref[...]
    split(sub)
    bcur[...] = jnp.zeros_like(bcur)
    br[...] = jnp.zeros_like(br)
    bet[...] = jnp.zeros_like(bet)
    hs[...] = jnp.zeros_like(hs)

    pl.semaphore_wait(barrier, 4 * (nz - 1) + plane - 1)

    def x_beside():
        return remote(xt_ref, xt4.at[:, own], x_ss.at[1], x_rs.at[1], sibling, v)

    def x_across():
        return remote(xt_ref, xt4.at[:, own], x_ss.at[2], x_rs.at[2], across, near)

    def x_relay():
        b = block(block_at(2))
        return remote(xt4.at[:, b], xt4.at[:, b], x_ss.at[3], x_rs.at[3], sibling, v)

    def x_from(i):
        b = block(block_at(i))
        return remote(xt_ref, xt4.at[:, b], x_ss.at[i], x_rs.at[i], sibling, v)

    def p_copy(j):
        rows = pl.ds(pl.multiple_of(j * 8, 8), 8)
        return remote(ybuf.at[rows], y4.at[:, own], p_ss.at[j], p_rs.at[sub], 4 * z + j, v)

    def p_from(j):
        rows = pl.ds(pl.multiple_of(j * 8, 8), 8)
        return remote(ybuf.at[rows], y4.at[:, block(j)], p_ss.at[j], p_rs.at[j], 4 * z + j, v)

    def y_copy(j):
        return remote(ybuf, yall.at[v], y_ss.at[j], y_rs.at[v], s, j)

    def y_from(j):
        return remote(ybuf, yall.at[j], y_ss.at[j], y_rs.at[j], s, j)

    def gr_copy(j):
        return remote(grs, grr.at[z], gr_ss.at[j], gr_rs.at[z], 4 * j + sub, v)

    def gr_from(j):
        return remote(grs, grr.at[j], gr_ss.at[j], gr_rs.at[j], 4 * j + sub, v)

    def h_copy(j):
        return remote(hs.at[j], hr.at[z], h_ss.at[j], h_rs.at[z], 4 * j + sub, v)

    def h_from(j):
        return remote(hs.at[j], hr.at[j], h_ss.at[j], h_rs.at[j], 4 * j + sub, v)

    def b_copy(j):
        return remote(br.at[z], br.at[z], b_ss.at[j], b_rs.at[z], 4 * j + sub, v)

    def b_from(j):
        return remote(br.at[z], br.at[j], b_ss.at[j], b_rs.at[j], 4 * j + sub, v)

    def c_copy(j):
        return remote(crs.at[j], crr.at[s], c_ss.at[j], c_rs.at[s], j, v)

    def c_from(j):
        return remote(crs.at[j], crr.at[j], c_ss.at[j], c_rs.at[j], j, v)

    def f_copy(j):
        return remote(cfall.at[s], cfall.at[s], f_ss.at[j], f_rs.at[s], j, v)

    def f_from(j):
        return remote(cfall.at[s], cfall.at[j], f_ss.at[j], f_rs.at[j], j, v)

    def v_copy(j):
        to = 4 * z + lax.rem(j, 4)
        mine = ball.at[place]
        return remote(mine, mine, v_ss.at[j], v_rs.at[place], to, j // 4)

    def v_from(j):
        to = 4 * z + lax.rem(j, 4)
        return remote(ball.at[place], ball.at[j], v_ss.at[j], v_rs.at[j], to, j // 4)

    x_across().start()
    x_beside().start()
    each(4, lambda i: block_at(i), lambda j: p_copy(j).start())

    def products():
        beta = bet[:, 0:64]
        b_hi = beta.astype(BF16).astype(F32)
        rest = beta - b_hi
        b_mid = rest.astype(BF16).astype(F32)
        none = jnp.zeros_like(beta)
        rows = jnp.concatenate([b_hi, b_mid, rest - b_mid, none], axis=0)
        rows = jnp.concatenate([rows, rows], axis=1).astype(BF16)
        eta = dot(rows, xhl[...])
        eta = eta[0:8] + eta[8:16] + eta[16:24]
        fitted = 1.0 / (1.0 + jnp.exp(-eta))
        coded = y4[...]
        seen = coded >= 0.0
        wbuf[...] = jnp.where(seen, fitted * (1.0 - fitted), 0.0)
        work = jnp.where(seen, coded - fitted, 0.0)
        r_hi = work.astype(BF16).astype(F32)
        rest = work - r_hi
        r_mid = rest.astype(BF16).astype(F32)
        none = jnp.zeros_like(work)
        lhs[512:544, :] = jnp.concatenate([r_hi, r_mid, rest - r_mid, none], axis=0).astype(BF16)

        @pl.loop(0, 16)
        def _(i):
            cols = pl.ds(pl.multiple_of(i * 512, 512), 512)
            table = xt4[:, cols]
            for p in range(8):
                lhs[p * 64 : (p + 1) * 64, cols] = (table * wbuf[p : p + 1, cols]).astype(BF16)

        hacc[...] = exact_t(lhs[...], xhl[...])

    def pack():
        def one(p):
            return fold(hacc[p * 64 : (p + 1) * 64, :])

        grads = fold(hacc[512:520, :] + hacc[520:528, :] + hacc[528:536, :])
        for j in range(nz):
            hs[j, 0:64, :] = jnp.where(low, one(j), one(j + nz))
            hs[j, 64:65, :] = jnp.where(low, grads[j : j + 1], grads[j + nz : j + nz + 1])

    def crosses():
        @pl.loop(0, 8)
        def _(t):
            out = dot(xhl[:, own], gbuf[:, pl.ds(pl.multiple_of(t * 256, 256), 256)])
            out = out[0:64] + out[64:128]
            crs[2 * t] = out[:, 0:128]
            crs[2 * t + 1] = out[:, 128:256]

    def upright():
        @pl.loop(0, 16)
        def _(i):
            at = pl.ds(pl.multiple_of(i * 128, 128), 128)
            from_ = pl.ds(pl.multiple_of(sub * 2048 + i * 128, 128), 128)
            both = xhl[:, from_].astype(F32).T.astype(BF16)
            x4[at, 0:128] = both
            x4[at, 128:256] = both

    def project(t):
        for h in range(2):
            part = cfall[2 * t + h]
            cols = slice(h * 128, (h + 1) * 128)
            c4[0:64, cols] = part[0:64]
            c4[64:128, cols] = part[0:64]
            c4[128:192, cols] = part[64:128]
            c4[192:256, cols] = part[64:128]
        cols = pl.ds(pl.multiple_of(t * PROJ, PROJ), PROJ)

        @pl.loop(0, 2048 // ROWS)
        def _(i):
            rows = pl.ds(pl.multiple_of(i * ROWS, ROWS), ROWS)
            proj = gbuf[rows, cols].astype(F32) - dot(x4[rows, :], c4[...])
            gbuf[rows, cols] = proj.astype(BF16)
            psq[rows, cols] = (proj * proj).astype(BF16)

    def send_sums():
        pack()
        each(nz, zpeer, lambda j: h_copy(j).start())

    def total_sums():
        each(nz, zpeer, lambda j: h_from(j).wait_recv())
        hr[z] = hs[z]
        total = hr[0]
        for j in range(1, nz):
            total = total + hr[j]
        return total

    def share(delta):
        bcur[0:1, :] = bcur[0:1, :] + delta
        br[z] = bcur[...]
        each(nz, zpeer, lambda j: b_copy(j).start())

    def collect():
        each(nz, zpeer, lambda j: b_from(j).wait_recv())
        rows = br[:, 0, :]
        bet[...] = jnp.concatenate([rows, pltpu.roll(rows, 64, 1)], axis=0)
        each(nz, zpeer, lambda j: h_copy(j).wait_send())

    gcopy.wait()
    crosses()
    upright()
    x_from(2).wait_recv()
    x_relay().start()
    x_from(1).wait_recv()
    split(block_at(1))
    split(block_at(2))
    each(4, lambda i: block_at(i), lambda j: p_from(j).wait_recv())
    x_from(3).wait_recv()
    split(block_at(3))
    products()
    send_sums()
    gram = exact_t(xhl[...], xhl[...])
    grs[...] = fold(gram[0:64, :] + gram[64:128, :])
    each(nz, zpeer, lambda j: gr_copy(j).start())
    each(ns, speer, lambda j: c_copy(j).start())
    each(nz, zpeer, lambda j: gr_from(j).wait_recv())
    grr[z] = grs[...]
    gram = grr[0]
    for j in range(1, nz):
        gram = gram + grr[j]
    ginv_ref[...] = sweep(gram, True)
    share(sweep(total_sums(), False))
    collect()

    @pl.loop(1, ITERS)
    def _(it):
        products()
        send_sums()

        @pl.when(it == 1)
        def _():
            each(ns, speer, lambda j: c_from(j).wait_recv())
            crr[s] = crs[s]
            cross = crr[0]
            for j in range(1, ns):
                cross = cross + crr[j]
            hi, lo = two(exact(-ginv_ref[:, 0:64], cross))
            cfall[s, 0:64, :] = hi
            cfall[s, 64:128, :] = lo
            each(ns, speer, lambda j: f_copy(j).start())
            each(nv, vpeer, lambda j: y_copy(j).start())

        @pl.when(it == 2)
        def _():
            each(ns, speer, lambda j: f_from(j).wait_recv())

        @pl.when(it >= 2)
        def _():
            @pl.loop((it - 2) * 4, (it - 1) * 4)
            def _(t):
                project(t)

        delta = sweep(total_sums(), False)
        each(nz, zpeer, lambda j: b_copy(j).wait_send())
        share(delta)
        collect()

    ball[place] = bet[...]
    each(plane, ppeer, lambda j: v_copy(j).start())
    each(nv, vpeer, lambda j: y_from(j).wait_recv())
    yall[v] = ybuf[...]
    each(plane, ppeer, lambda j: v_from(j).wait_recv())

    @pl.loop(0, nv)
    def _(u):
        rows = ball[pl.ds(u * 4, 4)].reshape(32, 128)
        eta = exact(rows[:, 0:64], xt_ref[...])
        fitted = 1.0 / (1.0 + jnp.exp(-eta))
        coded = yall[u]
        seen = coded >= 0.0
        resid = jnp.where(seen, coded - fitted, 0.0).astype(BF16)
        wslab = jnp.where(seen, fitted * (1.0 - fitted), 0.0).astype(BF16)
        wide = resid.astype(F32)
        square = (wide * wide).astype(BF16)
        for h in range(2):
            half = slice(h * 16, (h + 1) * 16)
            at = pl.multiple_of(u * 16 + h * 128, 16)
            r1[pl.ds(at, 16), :] = resid[half]
            r2[pl.ds(at, 16), :] = square[half]
            r2[pl.ds(at + 256, 16), :] = wslab[half]

    width = 2048 // TILES

    def a_copy(t):
        return remote(asd.at[t], arv.at[t], a_ss.at[t], a_rs.at[t], s + 1 - 2 * core, v)

    def q_copy(t, q):
        return remote(bsd.at[t, q], brv.at[t, myq], q_ss.at[t, q], q_rs.at[t, myq], 2 * q + core, v)

    def q_from(t, q):
        return remote(bsd.at[t, q], brv.at[t, q], q_ss.at[t, q], q_rs.at[t, q], 2 * q + core, v)

    def others(do):
        @pl.loop(1, ns // 2)
        def _(d):
            do(lax.rem(myq + d, ns // 2))

    @pl.loop(0, TILES + 1)
    def _(t):
        @pl.when(t < TILES)
        def _():
            slot = lax.rem(t, 2)
            cols = pl.ds(pl.multiple_of(t * width, width), width)
            so[slot, 0:256, :] = dot(r1[...], gbuf[:, cols])
            so[slot, 256:768, :] = dot(r2[...], psq[:, cols])

            @pl.loop(0, ns // 2)
            def _(q):
                at = pl.multiple_of((1 - core) * 128 + q * 16, 16)
                hi, lo = two(so[slot, pl.ds(at, 16), :])
                asd[t, q, 0:16, :] = hi
                asd[t, q, 16:32, :] = lo
                asd[t, q, 32:48, :] = so[slot, pl.ds(at + 256, 16), :].astype(BF16)
                asd[t, q, 48:64, :] = so[slot, pl.ds(at + 512, 16), :].astype(BF16)

            a_copy(t).start()

        @pl.when(t > 0)
        def _():
            b = t - 1
            slot = lax.rem(b, 2)
            a_copy(b).wait_recv()

            def total(q):
                at = pl.multiple_of(core * 128 + q * 16, 16)
                score = so[slot, pl.ds(at, 16), :]
                score = score + arv[b, q, 0:16, :].astype(F32) + arv[b, q, 16:32, :].astype(F32)
                robust = so[slot, pl.ds(at + 256, 16), :] + arv[b, q, 32:48, :].astype(F32)
                model = so[slot, pl.ds(at + 512, 16), :] + arv[b, q, 48:64, :].astype(F32)
                return score, robust, model

            def send(q):
                score, robust, model = total(q)
                hi, lo = two(score)
                bsd[b, q, 0:16, :] = hi
                bsd[b, q, 16:32, :] = lo
                bsd[b, q, 32:48, :] = robust.astype(BF16)
                bsd[b, q, 48:64, :] = model.astype(BF16)
                q_copy(b, q).start()

            others(send)
            score, robust, model = total(myq)
            fin[b, 0:16, :] = score
            fin[b, 16:32, :] = robust
            fin[b, 32:48, :] = model

    for t in range(TILES):
        others(lambda q: q_from(t, q).wait_recv())
        brv[t, myq] = jnp.zeros((64, width), BF16)
        score, robust, model = fin[t, 0:16, :], fin[t, 16:32, :], fin[t, 32:48, :]
        for q in range(ns // 2):
            score = score + brv[t, q, 0:16, :].astype(F32) + brv[t, q, 16:32, :].astype(F32)
            robust = robust + brv[t, q, 32:48, :].astype(F32)
            model = model + brv[t, q, 48:64, :].astype(F32)
        cols = slice(t * width, (t + 1) * width)
        tot_ref[0:16, cols] = score
        tot_ref[16:32, cols] = robust
        tot_ref[32:48, cols] = model

    x_across().wait_send()
    x_beside().wait_send()
    x_relay().wait_send()
    each(4, lambda i: block_at(i), lambda j: p_copy(j).wait_send())
    each(nz, zpeer, lambda j: b_copy(j).wait_send())
    each(nz, zpeer, lambda j: gr_copy(j).wait_send())
    each(ns, speer, lambda j: c_copy(j).wait_send())
    each(ns, speer, lambda j: f_copy(j).wait_send())
    each(nv, vpeer, lambda j: y_copy(j).wait_send())
    each(plane, ppeer, lambda j: v_copy(j).wait_send())

    @pl.loop(0, TILES)
    def _(t):
        a_copy(t).wait_send()
        others(lambda q: q_copy(t, q).wait_send())


def per_device(ns, nv, genotype, covariates, outcome, cohort, measured):
    vm = pltpu.VMEM
    dma = pltpu.SemaphoreType.DMA
    width = 2048 // TILES
    nz = ns // 4
    scratch = [
        vm((2048, 2048), BF16),
        vm((2048, 2048), BF16),
        vm((64, 8192), F32),
        vm((128, 8192), BF16),
        vm((2048, 256), BF16),
        vm((32, 2048), F32),
        vm((8, 8192), F32),
        vm((nv, 32, 2048), F32),
        vm((8, 8192), F32),
        vm((544, 8192), BF16),
        vm((544, 128), F32),
        vm((nz, 72, 128), F32),
        vm((nz, 72, 128), F32),
        vm((ns, 64, 128), F32),
        vm((ns, 64, 128), F32),
        vm((64, 128), F32),
        vm((nz, 64, 128), F32),
        vm((64, 128), F32),
        vm((8, 128), F32),
        vm((nz, 8, 128), F32),
        vm((8, 128), F32),
        vm((4 * nv, 8, 128), F32),
        vm((256, PROJ), BF16),
        vm((ns, 128, 128), BF16),
        vm((256, 2048), BF16),
        vm((512, 2048), BF16),
        vm((2, 768, width), F32),
        vm((TILES, ns // 2, 64, width), BF16),
        vm((TILES, ns // 2, 64, width), BF16),
        vm((TILES, ns // 2, 64, width), BF16),
        vm((TILES, ns // 2, 64, width), BF16),
        vm((TILES, 48, width), F32),
        dma,
    ]
    scratch += [dma((ns,))] * 4 + [dma((nz,))] * 6 + [dma((4,))] * 4 + [dma((nv,))] * 2
    scratch += [dma((4 * nv,))] * 2 + [dma((TILES,))] * 2 + [dma((TILES, ns // 2))] * 2
    inside = pl.BlockSpec(memory_space=pltpu.VMEM)
    totals = pl.pallas_call(
        functools.partial(kernel, ns, nv),
        out_shape=jax.ShapeDtypeStruct((48, 2048), F32),
        in_specs=[pl.BlockSpec(memory_space=pl.ANY)] + [inside] * 4,
        out_specs=inside,
        scratch_shapes=scratch,
        compiler_params=pltpu.CompilerParams(
            collective_id=0, has_side_effects=True, vmem_limit_bytes=60 * 2**20
        ),
        name="score_tests",
    )(genotype, covariates.T, outcome.T, cohort[None, :], measured.T)
    score, robust, model = totals[0:16], totals[16:32], totals[32:48]
    return score * lax.rsqrt(robust + EPS), score * lax.rsqrt(model + EPS)


def solution(mesh):
    placed = (
        P("sample", "variant"),
        P("sample", None),
        P("sample", "variant"),
        P("sample"),
        P("variant", None),
    )
    return jax.shard_map(
        functools.partial(per_device, mesh.shape["sample"], mesh.shape["variant"]),
        mesh=mesh,
        in_specs=placed,
        out_specs=(P("sample", "variant"), P("sample", "variant")),
        check_vma=False,
    )
```

time: 201 us -> 140 us (0.70)
  Pallas kernels: 191 us -> 137 us
  local copies, waits for them, and re-layouts: 3.82 us -> 0 us
  other arithmetic: 4.08 us -> 1.77 us
    pallas_call x1, Pallas kernels: 191 us -> 137 us  [per_device(): pl.pallas_call(functools.partial(kernel, ns, nv), out_shape=jax.ShapeDtyp...]
    unnamed x11 -> x0, local copies, waits for them, and re-layouts: 3.49 us -> none
    concatenate x2 -> x0, other arithmetic: 2.8 us -> none  [the longest x1 1.71 us: per_device(): x4 = jnp.concatenate([xh, xl, xh, xl], axis=1).astype(BF16)]
where the time goes in v2:
time: 140 us; the launch traced here: 139 us
  Pallas kernels  137 us (98%)
  other arithmetic  1.77 us (1%)
    pallas_call x1, Pallas kernels, per_device(): pl.pallas_call(functools.partial(kernel, ns, nv), out_shape=jax.ShapeDtyp...  137 us

profile of v2, /device:TPU:0, one launch (start us, length us, event | category | flops | bytes accessed | tf_op | source)
XLA Modules:
  0.0 139.1 jit_solution(13157916404262294992)
XLA Ops:
  0.6 136.7 %score_tests.1 = f32[48,2048]{1,0:T(8,128)} custom-call(bf16[2048,2048]{1,0:T(8,128)(2,1)} %g_hbm.1, f32[64,2048]{1,0:T(8,128)} %bitcast.4, f32[32,2048]{1,0:T(8,128)} %bitcast.5, s32[1,2048]{1,0:T(1,128)} %bitcast.6, s32[16,32]{1,0:T(8,128)} %bitcast.7), custom_call_target="tpu_custom_call" | custom-call | tf_op jit(solution)/shard_map/score_tests/pallas_call | solution.py:641
  137.3 1.8 %rsqrt_multiply_fusion = (f32[16,2048]{1,0:T(8,128)}, f32[16,2048]{1,0:T(8,128)}) fusion(f32[48,2048]{1,0:T(8,128)} %score_tests.1), kind=kLoop, calls=%fused_computation | loop fusion | flops 131072 | bytes 655360 | tf_op jit(solution)/shard_map/mul | solution.py:653

commit v3 on v2

--- a/solution.py
+++ b/solution.py
@@ -150,6 +150,8 @@
     b_rs,
     x_ss,
     x_rs,
+    l_ss,
+    l_rs,
     p_ss,
     p_rs,
     y_ss,
@@ -160,6 +162,7 @@
     a_rs,
     q_ss,
     q_rs,
+    told,
 ):
     nz = ns // 4
     s = lax.axis_index("sample")
@@ -186,6 +189,9 @@
         xhl[0:64, block(b)] = hi
         xhl[64:128, block(b)] = lo
 
+    def join(b):
+        xt4[:, block(b)] = xhl[0:64, block(b)].astype(F32) + xhl[64:128, block(b)].astype(F32)
+
     def block_at(i):
         return 2 * lax.rem(xh + i // 2, 2) + lax.rem(core + i, 2)
 
@@ -224,12 +230,13 @@
     def ppeer(d):
         return lax.rem(place + d, plane)
 
-    @pl.loop(1, nz)
-    def _(d):
-        for k in range(4):
-            greet(4 * zpeer(d) + k, v)
-
-    each(plane, ppeer, lambda j: greet(4 * z + lax.rem(j, 4), j // 4))
+    greet(across, near)
+    for d in (1, 2, 3):
+        greet(4 * z + lax.rem(sub + d, 4), v)
+    for d in (2, 1, 3):
+        greet(4 * zpeer(d) + sub, v)
+    for d in range(2, nv, 2):
+        greet(s, vpeer(d))
 
     hot = lax.broadcasted_iota(jnp.int32, (16, 2048), 0) == cohort_ref[...]
     mask = lax.dot_general(
@@ -248,21 +255,29 @@
     bet[...] = jnp.zeros_like(bet)
     hs[...] = jnp.zeros_like(hs)
 
-    pl.semaphore_wait(barrier, 4 * (nz - 1) + plane - 1)
-
-    def x_beside():
-        return remote(xt_ref, xt4.at[:, own], x_ss.at[1], x_rs.at[1], sibling, v)
-
-    def x_across():
-        return remote(xt_ref, xt4.at[:, own], x_ss.at[2], x_rs.at[2], across, near)
-
-    def x_relay():
-        b = block(block_at(2))
-        return remote(xt4.at[:, b], xt4.at[:, b], x_ss.at[3], x_rs.at[3], sibling, v)
-
-    def x_from(i):
-        b = block(block_at(i))
-        return remote(xt_ref, xt4.at[:, b], x_ss.at[i], x_rs.at[i], sibling, v)
+    pl.semaphore_wait(barrier, 7 + nv // 2 - 1)
+
+    def part(low_part, b):
+        return xhl.at[pl.ds(64 * low_part, 64), block(b)]
+
+    def x_sems(low_part, i):
+        return (l_ss.at[i], l_rs.at[i]) if low_part else (x_ss.at[i], x_rs.at[i])
+
+    def x_beside(low_part):
+        mine = part(low_part, sub)
+        return remote(mine, mine, *x_sems(low_part, 1), sibling, v)
+
+    def x_across(low_part):
+        mine = part(low_part, sub)
+        return remote(mine, mine, *x_sems(low_part, 2), across, near)
+
+    def x_relay(low_part):
+        theirs = part(low_part, block_at(2))
+        return remote(theirs, theirs, *x_sems(low_part, 3), sibling, v)
+
+    def x_from(low_part, i):
+        theirs = part(low_part, block_at(i))
+        return remote(theirs, theirs, *x_sems(low_part, i), sibling, v)
 
     def p_copy(j):
         rows = pl.ds(pl.multiple_of(j * 8, 8), 8)
@@ -317,8 +332,8 @@
         to = 4 * z + lax.rem(j, 4)
         return remote(ball.at[place], ball.at[j], v_ss.at[j], v_rs.at[j], to, j // 4)
 
-    x_across().start()
-    x_beside().start()
+    x_across(0).start()
+    x_beside(0).start()
     each(4, lambda i: block_at(i), lambda j: p_copy(j).start())
 
     def products():
@@ -349,16 +364,44 @@
             for p in range(8):
                 lhs[p * 64 : (p + 1) * 64, cols] = (table * wbuf[p : p + 1, cols]).astype(BF16)
 
-        hacc[...] = exact_t(lhs[...], xhl[...])
-
-    def pack():
-        def one(p):
-            return fold(hacc[p * 64 : (p + 1) * 64, :])
-
-        grads = fold(hacc[512:520, :] + hacc[520:528, :] + hacc[528:536, :])
-        for j in range(nz):
-            hs[j, 0:64, :] = jnp.where(low, one(j), one(j + nz))
-            hs[j, 64:65, :] = jnp.where(low, grads[j : j + 1], grads[j + nz : j + nz + 1])
+        hacc[...] = fold(exact_t(lhs[...], xhl[...]))
+
+    def products0():
+        coded = y4[...]
+        seen = coded >= 0.0
+        wbuf[...] = jnp.where(seen, 0.25, 0.0)
+        work = jnp.where(seen, coded - 0.5, 0.0)
+        r_hi = work.astype(BF16).astype(F32)
+        rest = work - r_hi
+        r_mid = rest.astype(BF16).astype(F32)
+        none = jnp.zeros_like(work)
+        lhs[512:544, :] = jnp.concatenate([r_hi, r_mid, rest - r_mid, none], axis=0).astype(BF16)
+
+        @pl.loop(0, 16)
+        def _(i):
+            cols = pl.ds(pl.multiple_of(i * 512, 512), 512)
+            table = xhl[0:64, cols].astype(F32)
+            for p in range(8):
+                lhs[p * 64 : (p + 1) * 64, cols] = (table * wbuf[p : p + 1, cols]).astype(BF16)
+
+        out = exact_t(lhs[...], xhl[0:64, :])
+        hacc[...] = jnp.concatenate([out, out], axis=1)
+
+    def send_sums():
+        grads = hacc[512:520, :] + hacc[520:528, :] + hacc[528:536, :]
+        line = lax.broadcasted_iota(jnp.int32, (4, 1), 0)
+
+        def one(j):
+            first = hacc[pl.ds(pl.multiple_of(j * 64, 64), 64), :]
+            second = hacc[pl.ds(pl.multiple_of((j + nz) * 64, 64), 64), :]
+            hs[j, 0:64, :] = jnp.where(low, first, second)
+            pair = jnp.where(low, grads[0:4], grads[4:8])
+            hs[j, 64:65, :] = jnp.sum(jnp.where(line == j, pair, 0.0), axis=0, keepdims=True)
+
+        for d in (2, 1, 3):
+            one(zpeer(d))
+            h_copy(zpeer(d)).start()
+        one(z)
 
     def crosses():
         @pl.loop(0, 8)
@@ -394,59 +437,85 @@
             gbuf[rows, cols] = proj.astype(BF16)
             psq[rows, cols] = (proj * proj).astype(BF16)
 
-    def send_sums():
-        pack()
-        each(nz, zpeer, lambda j: h_copy(j).start())
-
     def total_sums():
-        each(nz, zpeer, lambda j: h_from(j).wait_recv())
-        hr[z] = hs[z]
-        total = hr[0]
-        for j in range(1, nz):
-            total = total + hr[j]
+        total = hs[z]
+        for d in (1, 3, 2):
+            h_from(zpeer(d)).wait_recv()
+            total = total + hr[zpeer(d)]
         return total
 
     def share(delta):
         bcur[0:1, :] = bcur[0:1, :] + delta
         br[z] = bcur[...]
-        each(nz, zpeer, lambda j: b_copy(j).start())
+        for d in (2, 1, 3):
+            b_copy(zpeer(d)).start()
 
     def collect():
-        each(nz, zpeer, lambda j: b_from(j).wait_recv())
+        for d in (1, 3, 2):
+            b_from(zpeer(d)).wait_recv()
         rows = br[:, 0, :]
         bet[...] = jnp.concatenate([rows, pltpu.roll(rows, 64, 1)], axis=0)
-        each(nz, zpeer, lambda j: h_copy(j).wait_send())
+        for d in (1, 2, 3):
+            h_copy(zpeer(d)).wait_send()
 
     gcopy.wait()
     crosses()
+    x_from(0, 2).wait_recv()
+    x_relay(0).start()
+    for d in (1, 2, 3):
+        pl.semaphore_signal(
+            told, inc=1, device_id=(4 * z + lax.rem(sub + d, 4), v), device_id_type=mesh_id
+        )
+    x_across(1).start()
+    x_beside(1).start()
     upright()
-    x_from(2).wait_recv()
-    x_relay().start()
-    x_from(1).wait_recv()
-    split(block_at(1))
-    split(block_at(2))
+    x_from(0, 1).wait_recv()
     each(4, lambda i: block_at(i), lambda j: p_from(j).wait_recv())
-    x_from(3).wait_recv()
-    split(block_at(3))
-    products()
+    x_from(0, 3).wait_recv()
+    products0()
     send_sums()
+    x_from(1, 2).wait_recv()
+    x_relay(1).start()
+    join(block_at(2))
+    x_from(1, 1).wait_recv()
+    join(block_at(1))
+    x_from(1, 3).wait_recv()
+    join(block_at(3))
+    pl.semaphore_wait(told, 3)
+    share(sweep(total_sums(), False))
     gram = exact_t(xhl[...], xhl[...])
     grs[...] = fold(gram[0:64, :] + gram[64:128, :])
-    each(nz, zpeer, lambda j: gr_copy(j).start())
+    for d in (2, 1, 3):
+        gr_copy(zpeer(d)).start()
+    collect()
     each(ns, speer, lambda j: c_copy(j).start())
-    each(nz, zpeer, lambda j: gr_from(j).wait_recv())
-    grr[z] = grs[...]
-    gram = grr[0]
-    for j in range(1, nz):
-        gram = gram + grr[j]
-    ginv_ref[...] = sweep(gram, True)
-    share(sweep(total_sums(), False))
-    collect()
 
     @pl.loop(1, ITERS)
     def _(it):
         products()
         send_sums()
+
+        @pl.when(it == 1)
+        def _():
+            gram = grs[...]
+            for d in (1, 3, 2):
+                gr_from(zpeer(d)).wait_recv()
+                gram = gram + grr[zpeer(d)]
+            ginv_ref[...] = sweep(gram, True)
+
+        @pl.when(it == 2)
+        def _():
+            each(ns, speer, lambda j: f_from(j).wait_recv())
+
+        @pl.when(it >= 2)
+        def _():
+            @pl.loop((it - 2) * 4, (it - 2) * 4 + 2)
+            def _(t):
+                project(t)
+
+        delta = sweep(total_sums(), False)
+        each(nz, zpeer, lambda j: b_copy(j).wait_send())
+        share(delta)
 
         @pl.when(it == 1)
         def _():
@@ -461,19 +530,12 @@
             each(ns, speer, lambda j: f_copy(j).start())
             each(nv, vpeer, lambda j: y_copy(j).start())
 
-        @pl.when(it == 2)
-        def _():
-            each(ns, speer, lambda j: f_from(j).wait_recv())
-
         @pl.when(it >= 2)
         def _():
-            @pl.loop((it - 2) * 4, (it - 1) * 4)
+            @pl.loop((it - 2) * 4 + 2, (it - 1) * 4)
             def _(t):
                 project(t)
 
-        delta = sweep(total_sums(), False)
-        each(nz, zpeer, lambda j: b_copy(j).wait_send())
-        share(delta)
         collect()
 
     ball[place] = bet[...]
@@ -552,11 +614,9 @@
 
             def send(q):
                 score, robust, model = total(q)
-                hi, lo = two(score)
-                bsd[b, q, 0:16, :] = hi
-                bsd[b, q, 16:32, :] = lo
-                bsd[b, q, 32:48, :] = robust.astype(BF16)
-                bsd[b, q, 48:64, :] = model.astype(BF16)
+                bsd[b, q, 0:16, :] = score.astype(BF16)
+                bsd[b, q, 16:32, :] = robust.astype(BF16)
+                bsd[b, q, 32:48, :] = model.astype(BF16)
                 q_copy(b, q).start()
 
             others(send)
@@ -565,22 +625,10 @@
             fin[b, 16:32, :] = robust
             fin[b, 32:48, :] = model
 
-    for t in range(TILES):
-        others(lambda q: q_from(t, q).wait_recv())
-        brv[t, myq] = jnp.zeros((64, width), BF16)
-        score, robust, model = fin[t, 0:16, :], fin[t, 16:32, :], fin[t, 32:48, :]
-        for q in range(ns // 2):
-            score = score + brv[t, q, 0:16, :].astype(F32) + brv[t, q, 16:32, :].astype(F32)
-            robust = robust + brv[t, q, 32:48, :].astype(F32)
-            model = model + brv[t, q, 48:64, :].astype(F32)
-        cols = slice(t * width, (t + 1) * width)
-        tot_ref[0:16, cols] = score
-        tot_ref[16:32, cols] = robust
-        tot_ref[32:48, cols] = model
-
-    x_across().wait_send()
-    x_beside().wait_send()
-    x_relay().wait_send()
+    for low_part in range(2):
+        x_across(low_part).wait_send()
+        x_beside(low_part).wait_send()
+        x_relay(low_part).wait_send()
     each(4, lambda i: block_at(i), lambda j: p_copy(j).wait_send())
     each(nz, zpeer, lambda j: b_copy(j).wait_send())
     each(nz, zpeer, lambda j: gr_copy(j).wait_send())
@@ -588,6 +636,19 @@
     each(ns, speer, lambda j: f_copy(j).wait_send())
     each(nv, vpeer, lambda j: y_copy(j).wait_send())
     each(plane, ppeer, lambda j: v_copy(j).wait_send())
+
+    for t in range(TILES):
+        others(lambda q: q_from(t, q).wait_recv())
+        brv[t, myq] = jnp.zeros((48, width), BF16)
+        score, robust, model = fin[t, 0:16, :], fin[t, 16:32, :], fin[t, 32:48, :]
+        for q in range(ns // 2):
+            score = score + brv[t, q, 0:16, :].astype(F32)
+            robust = robust + brv[t, q, 16:32, :].astype(F32)
+            model = model + brv[t, q, 32:48, :].astype(F32)
+        cols = slice(t * width, (t + 1) * width)
+        tot_ref[0:16, cols] = score
+        tot_ref[16:32, cols] = robust
+        tot_ref[32:48, cols] = model
 
     @pl.loop(0, TILES)
     def _(t):
@@ -630,13 +691,14 @@
         vm((2, 768, width), F32),
         vm((TILES, ns // 2, 64, width), BF16),
         vm((TILES, ns // 2, 64, width), BF16),
-        vm((TILES, ns // 2, 64, width), BF16),
-        vm((TILES, ns // 2, 64, width), BF16),
+        vm((TILES, ns // 2, 48, width), BF16),
+        vm((TILES, ns // 2, 48, width), BF16),
         vm((TILES, 48, width), F32),
         dma,
     ]
-    scratch += [dma((ns,))] * 4 + [dma((nz,))] * 6 + [dma((4,))] * 4 + [dma((nv,))] * 2
+    scratch += [dma((ns,))] * 4 + [dma((nz,))] * 6 + [dma((4,))] * 6 + [dma((nv,))] * 2
     scratch += [dma((4 * nv,))] * 2 + [dma((TILES,))] * 2 + [dma((TILES, ns // 2))] * 2
+    scratch.append(pltpu.SemaphoreType.REGULAR)
     inside = pl.BlockSpec(memory_space=pltpu.VMEM)
     totals = pl.pallas_call(
         functools.partial(kernel, ns, nv),

time: 140 us -> 118 us (0.84)
  Pallas kernels: 137 us -> 115 us
    pallas_call x1, Pallas kernels: 137 us -> 115 us  [per_device(): pl.pallas_call(functools.partial(kernel, ns, nv), out_shape=jax.ShapeDtyp...]
where the time goes in v3:
time: 118 us; the launch traced here: 117 us
  Pallas kernels  115 us (97%)
  other arithmetic  1.77 us (2%)
    pallas_call x1, Pallas kernels, per_device(): pl.pallas_call(functools.partial(kernel, ns, nv), out_shape=jax.ShapeDtyp...  115 us

profile of v3, /device:TPU:0, one launch (start us, length us, event | category | flops | bytes accessed | tf_op | source)
XLA Modules:
  0.0 117.3 jit_solution(16816120204333427281)
XLA Ops:
  0.6 114.9 %score_tests.1 = f32[48,2048]{1,0:T(8,128)} custom-call(bf16[2048,2048]{1,0:T(8,128)(2,1)} %g_hbm.1, f32[64,2048]{1,0:T(8,128)} %bitcast.4, f32[32,2048]{1,0:T(8,128)} %bitcast.5, s32[1,2048]{1,0:T(1,128)} %bitcast.6, s32[16,32]{1,0:T(8,128)} %bitcast.7), custom_call_target="tpu_custom_call" | custom-call | tf_op jit(solution)/shard_map/score_tests/pallas_call | solution.py:703
  115.6 1.8 %rsqrt_multiply_fusion = (f32[16,2048]{1,0:T(8,128)}, f32[16,2048]{1,0:T(8,128)}) fusion(f32[48,2048]{1,0:T(8,128)} %score_tests.1), kind=kLoop, calls=%fused_computation | loop fusion | flops 131072 | bytes 655360 | tf_op jit(solution)/shard_map/mul | solution.py:715

commit v4 on v3

--- a/solution.py
+++ b/solution.py
@@ -12,7 +12,8 @@
 HIGHEST = lax.Precision.HIGHEST
 F32 = jnp.float32
 BF16 = jnp.bfloat16
-TILES = 4
+LAG = 6
+TILES = 8
 PROJ = 256
 ROWS = 512
 
@@ -120,6 +121,8 @@
     hr,
     crs,
     crr,
+    cmid,
+    crt,
     grs,
     grr,
     ginv_ref,
@@ -136,6 +139,9 @@
     arv,
     bsd,
     brv,
+    keep,
+    lsd,
+    lrv,
     fin,
     g_sem,
     c_ss,
@@ -162,6 +168,8 @@
     a_rs,
     q_ss,
     q_rs,
+    w_ss,
+    w_rs,
     told,
 ):
     nz = ns // 4
@@ -171,7 +179,6 @@
     sub = lax.rem(s, 4)
     core = lax.rem(s, 2)
     xh = sub // 2
-    myq = s // 2
     sibling = s + 1 - 2 * core
     across = s + 2 - 4 * xh
     near = v + 1 - 2 * lax.rem(v, 2)
@@ -194,9 +201,6 @@
 
     def block_at(i):
         return 2 * lax.rem(xh + i // 2, 2) + lax.rem(core + i, 2)
-
-    def speer(d):
-        return lax.rem(s + d, ns)
 
     def zpeer(d):
         return lax.rem(z + d, nz)
@@ -311,17 +315,35 @@
     def b_from(j):
         return remote(br.at[z], br.at[j], b_ss.at[j], b_rs.at[j], 4 * j + sub, v)
 
-    def c_copy(j):
-        return remote(crs.at[j], crr.at[s], c_ss.at[j], c_rs.at[s], j, v)
-
-    def c_from(j):
-        return remote(crs.at[j], crr.at[j], c_ss.at[j], c_rs.at[j], j, v)
-
-    def f_copy(j):
-        return remote(cfall.at[s], cfall.at[s], f_ss.at[j], f_rs.at[s], j, v)
-
-    def f_from(j):
-        return remote(cfall.at[s], cfall.at[j], f_ss.at[j], f_rs.at[j], j, v)
+    def c1(j):
+        return remote(crs.at[pl.ds(4 * j, 4)], crr.at[pl.ds(4 * z, 4)], c_ss.at[j], c_rs.at[z], 4 * j + sub, v)
+
+    def c1_from(j):
+        four = pl.ds(4 * j, 4)
+        return remote(crs.at[four], crr.at[four], c_ss.at[j], c_rs.at[j], 4 * j + sub, v)
+
+    def c2(k):
+        return remote(cmid.at[k], crt.at[sub], c_ss.at[4 + k], c_rs.at[4 + sub], 4 * z + k, v)
+
+    def c2_from(k):
+        return remote(cmid.at[k], crt.at[k], c_ss.at[4 + k], c_rs.at[4 + k], 4 * z + k, v)
+
+    def f1(k):
+        return remote(cfall.at[s], cfall.at[s], f_ss.at[k], f_rs.at[sub], 4 * z + k, v)
+
+    def f1_from(k):
+        return remote(cfall.at[s], cfall.at[4 * z + k], f_ss.at[k], f_rs.at[k], 4 * z + k, v)
+
+    def f2(j):
+        four = cfall.at[pl.ds(4 * z, 4)]
+        return remote(four, four, f_ss.at[4 + j], f_rs.at[4 + z], 4 * j + sub, v)
+
+    def f2_from(j):
+        four = cfall.at[pl.ds(4 * j, 4)]
+        return remote(four, four, f_ss.at[4 + j], f_rs.at[4 + j], 4 * j + sub, v)
+
+    def beside(d):
+        return lax.rem(sub + d, 4)
 
     def v_copy(j):
         to = 4 * z + lax.rem(j, 4)
@@ -366,26 +388,27 @@
 
         hacc[...] = fold(exact_t(lhs[...], xhl[...]))
 
-    def products0():
-        coded = y4[...]
+    def products0(side):
+        wide = pl.ds(pl.multiple_of(side * 4096, 4096), 4096)
+        coded = y4[:, wide]
         seen = coded >= 0.0
-        wbuf[...] = jnp.where(seen, 0.25, 0.0)
+        wbuf[:, wide] = jnp.where(seen, 0.25, 0.0)
         work = jnp.where(seen, coded - 0.5, 0.0)
         r_hi = work.astype(BF16).astype(F32)
         rest = work - r_hi
         r_mid = rest.astype(BF16).astype(F32)
         none = jnp.zeros_like(work)
-        lhs[512:544, :] = jnp.concatenate([r_hi, r_mid, rest - r_mid, none], axis=0).astype(BF16)
-
-        @pl.loop(0, 16)
+        lhs[512:544, wide] = jnp.concatenate([r_hi, r_mid, rest - r_mid, none], axis=0).astype(BF16)
+
+        @pl.loop(0, 8)
         def _(i):
-            cols = pl.ds(pl.multiple_of(i * 512, 512), 512)
+            cols = pl.ds(pl.multiple_of(side * 4096 + i * 512, 512), 512)
             table = xhl[0:64, cols].astype(F32)
             for p in range(8):
                 lhs[p * 64 : (p + 1) * 64, cols] = (table * wbuf[p : p + 1, cols]).astype(BF16)
 
-        out = exact_t(lhs[...], xhl[0:64, :])
-        hacc[...] = jnp.concatenate([out, out], axis=1)
+        out = exact_t(lhs[:, wide], xhl[0:64, wide])
+        return jnp.concatenate([out, out], axis=1)
 
     def send_sums():
         grads = hacc[512:520, :] + hacc[520:528, :] + hacc[528:536, :]
@@ -460,6 +483,9 @@
 
     gcopy.wait()
     crosses()
+    x_from(0, 1).wait_recv()
+    p_from(block_at(1)).wait_recv()
+    hacc[...] = products0(xh)
     x_from(0, 2).wait_recv()
     x_relay(0).start()
     for d in (1, 2, 3):
@@ -469,10 +495,10 @@
     x_across(1).start()
     x_beside(1).start()
     upright()
-    x_from(0, 1).wait_recv()
-    each(4, lambda i: block_at(i), lambda j: p_from(j).wait_recv())
+    p_from(block_at(2)).wait_recv()
+    p_from(block_at(3)).wait_recv()
     x_from(0, 3).wait_recv()
-    products0()
+    hacc[...] += products0(1 - xh)
     send_sums()
     x_from(1, 2).wait_recv()
     x_relay(1).start()
@@ -488,7 +514,8 @@
     for d in (2, 1, 3):
         gr_copy(zpeer(d)).start()
     collect()
-    each(ns, speer, lambda j: c_copy(j).start())
+    for d in (2, 1, 3):
+        c1(zpeer(d)).start()
 
     @pl.loop(1, ITERS)
     def _(it):
@@ -502,14 +529,22 @@
                 gr_from(zpeer(d)).wait_recv()
                 gram = gram + grr[zpeer(d)]
             ginv_ref[...] = sweep(gram, True)
-
-        @pl.when(it == 2)
-        def _():
-            each(ns, speer, lambda j: f_from(j).wait_recv())
-
-        @pl.when(it >= 2)
-        def _():
-            @pl.loop((it - 2) * 4, (it - 2) * 4 + 2)
+            for d in (1, 3, 2):
+                c1_from(zpeer(d)).wait_recv()
+            for k in range(4):
+                piece = crs[4 * z + k]
+                for d in (1, 3, 2):
+                    piece = piece + crr[4 * zpeer(d) + k]
+                cmid[k] = piece
+            for d in (1, 2, 3):
+                c2(beside(d)).start()
+
+        @pl.when(it == 3)
+        def _():
+            for d in (1, 3, 2):
+                f2_from(zpeer(d)).wait_recv()
+
+            @pl.loop(0, 3)
             def _(t):
                 project(t)
 
@@ -519,20 +554,27 @@
 
         @pl.when(it == 1)
         def _():
-            each(ns, speer, lambda j: c_from(j).wait_recv())
-            crr[s] = crs[s]
-            cross = crr[0]
-            for j in range(1, ns):
-                cross = cross + crr[j]
+            cross = cmid[sub]
+            for d in (1, 2, 3):
+                c2_from(beside(d)).wait_recv()
+                cross = cross + crt[beside(d)]
             hi, lo = two(exact(-ginv_ref[:, 0:64], cross))
             cfall[s, 0:64, :] = hi
             cfall[s, 64:128, :] = lo
-            each(ns, speer, lambda j: f_copy(j).start())
+            for d in (1, 2, 3):
+                f1(beside(d)).start()
             each(nv, vpeer, lambda j: y_copy(j).start())
 
-        @pl.when(it >= 2)
-        def _():
-            @pl.loop((it - 2) * 4 + 2, (it - 1) * 4)
+        @pl.when(it == 2)
+        def _():
+            for d in (1, 2, 3):
+                f1_from(beside(d)).wait_recv()
+            for d in (2, 1, 3):
+                f2(zpeer(d)).start()
+
+        @pl.when(it == 3)
+        def _():
+            @pl.loop(3, 6)
             def _(t):
                 project(t)
 
@@ -540,12 +582,27 @@
 
     ball[place] = bet[...]
     each(plane, ppeer, lambda j: v_copy(j).start())
-    each(nv, vpeer, lambda j: y_from(j).wait_recv())
     yall[v] = ybuf[...]
-    each(plane, ppeer, lambda j: v_from(j).wait_recv())
+
+    @pl.loop(6, 8)
+    def _(t):
+        project(t)
 
     @pl.loop(0, nv)
-    def _(u):
+    def _(d):
+        u = lax.rem(v + nv - d, nv)
+
+        @pl.when(d == 0)
+        def _():
+            for k in (1, 2, 3):
+                v_from(4 * v + lax.rem(sub + k, 4)).wait_recv()
+
+        @pl.when(d > 0)
+        def _():
+            y_from(u).wait_recv()
+            for k in range(4):
+                v_from(4 * u + k).wait_recv()
+
         rows = ball[pl.ds(u * 4, 4)].reshape(32, 128)
         eta = exact(rows[:, 0:64], xt_ref[...])
         fitted = 1.0 / (1.0 + jnp.exp(-eta))
@@ -567,18 +624,91 @@
     def a_copy(t):
         return remote(asd.at[t], arv.at[t], a_ss.at[t], a_rs.at[t], s + 1 - 2 * core, v)
 
-    def q_copy(t, q):
-        return remote(bsd.at[t, q], brv.at[t, myq], q_ss.at[t, q], q_rs.at[t, myq], 2 * q + core, v)
-
-    def q_from(t, q):
-        return remote(bsd.at[t, q], brv.at[t, q], q_ss.at[t, q], q_rs.at[t, q], 2 * q + core, v)
-
-    def others(do):
-        @pl.loop(1, ns // 2)
-        def _(d):
-            do(lax.rem(myq + d, ns // 2))
-
-    @pl.loop(0, TILES + 1)
+    def z1(t, j):
+        pair = bsd.at[t, pl.ds(2 * j, 2)]
+        return remote(pair, brv.at[t, pl.ds(2 * z, 2)], q_ss.at[t, j], q_rs.at[t, z], 4 * j + sub, v)
+
+    def z1_from(t, j):
+        pair = bsd.at[t, pl.ds(2 * j, 2)]
+        return remote(pair, brv.at[t, pl.ds(2 * j, 2)], q_ss.at[t, j], q_rs.at[t, j], 4 * j + sub, v)
+
+    def x1(t):
+        four = pl.ds(4 * (1 - xh), 4)
+        return remote(bsd.at[t, four], brv.at[t, four], q_ss.at[t, 4], q_rs.at[t, 4], across, v)
+
+    def x1_from(t):
+        four = pl.ds(4 * xh, 4)
+        return remote(bsd.at[t, four], brv.at[t, four], q_ss.at[t, 4], q_rs.at[t, 4], across, v)
+
+    def x2(t):
+        return remote(lsd.at[t, 0], lrv.at[t, 0], w_ss.at[t, 4], w_rs.at[t, 4], across, v)
+
+    def z2(t, j):
+        return remote(lsd.at[t, j], lrv.at[t, z], w_ss.at[t, j], w_rs.at[t, z], 4 * j + sub, v)
+
+    def z2_from(t, j):
+        return remote(lsd.at[t, j], lrv.at[t, j], w_ss.at[t, j], w_rs.at[t, j], 4 * j + sub, v)
+
+    def stage1(b):
+        slot = lax.rem(b, 2)
+        a_copy(b).wait_recv()
+
+        def total(zz, xx):
+            at = pl.multiple_of(core * 128 + (2 * zz + xx) * 16, 16)
+            other = arv[b, 2 * zz + xx].astype(F32)
+            score = so[slot, pl.ds(at, 16), :] + other[0:16] + other[16:32]
+            robust = so[slot, pl.ds(at + 256, 16), :] + other[32:48]
+            model = so[slot, pl.ds(at + 512, 16), :] + other[48:64]
+            return jnp.concatenate([score, robust, model], axis=0)
+
+        @pl.when(lax.rem(b, 2) == 0)
+        def _():
+            for d in (2, 1, 3):
+                j = zpeer(d)
+                for xx in range(2):
+                    bsd[b, 2 * j + xx] = total(j, xx).astype(BF16)
+                z1(b, j).start()
+            for xx in range(2):
+                keep[b, xx] = total(z, xx)
+
+        @pl.when(lax.rem(b, 2) == 1)
+        def _():
+            for j in range(nz):
+                bsd[b, 4 * (1 - xh) + j] = total(j, 1 - xh).astype(BF16)
+            x1(b).start()
+            for j in range(nz):
+                keep[b, j] = total(j, xh)
+
+    def stage2(b):
+        @pl.when(lax.rem(b, 2) == 0)
+        def _():
+            for d in (1, 3, 2):
+                z1_from(b, zpeer(d)).wait_recv()
+
+            def total(xx):
+                out = keep[b, xx]
+                for d in (1, 2, 3):
+                    out = out + brv[b, 2 * zpeer(d) + xx].astype(F32)
+                return out
+
+            lsd[b, 0] = total(1 - xh).astype(BF16)
+            x2(b).start()
+            fin[b] = total(xh)
+
+        @pl.when(lax.rem(b, 2) == 1)
+        def _():
+            x1_from(b).wait_recv()
+
+            def total(j):
+                return keep[b, j] + brv[b, 4 * xh + j].astype(F32)
+
+            for d in (2, 1, 3):
+                j = zpeer(d)
+                lsd[b, j] = total(j).astype(BF16)
+                z2(b, j).start()
+            fin[b] = total(z)
+
+    @pl.loop(0, TILES + LAG)
     def _(t):
         @pl.when(t < TILES)
         def _():
@@ -598,32 +728,13 @@
 
             a_copy(t).start()
 
-        @pl.when(t > 0)
-        def _():
-            b = t - 1
-            slot = lax.rem(b, 2)
-            a_copy(b).wait_recv()
-
-            def total(q):
-                at = pl.multiple_of(core * 128 + q * 16, 16)
-                score = so[slot, pl.ds(at, 16), :]
-                score = score + arv[b, q, 0:16, :].astype(F32) + arv[b, q, 16:32, :].astype(F32)
-                robust = so[slot, pl.ds(at + 256, 16), :] + arv[b, q, 32:48, :].astype(F32)
-                model = so[slot, pl.ds(at + 512, 16), :] + arv[b, q, 48:64, :].astype(F32)
-                return score, robust, model
-
-            def send(q):
-                score, robust, model = total(q)
-                bsd[b, q, 0:16, :] = score.astype(BF16)
-                bsd[b, q, 16:32, :] = robust.astype(BF16)
-                bsd[b, q, 32:48, :] = model.astype(BF16)
-                q_copy(b, q).start()
-
-            others(send)
-            score, robust, model = total(myq)
-            fin[b, 0:16, :] = score
-            fin[b, 16:32, :] = robust
-            fin[b, 32:48, :] = model
+        @pl.when((t > 0) & (t <= TILES))
+        def _():
+            stage1(t - 1)
+
+        @pl.when(t >= LAG)
+        def _():
+            stage2(t - LAG)
 
     for low_part in range(2):
         x_across(low_part).wait_send()
@@ -632,28 +743,35 @@
     each(4, lambda i: block_at(i), lambda j: p_copy(j).wait_send())
     each(nz, zpeer, lambda j: b_copy(j).wait_send())
     each(nz, zpeer, lambda j: gr_copy(j).wait_send())
-    each(ns, speer, lambda j: c_copy(j).wait_send())
-    each(ns, speer, lambda j: f_copy(j).wait_send())
+    for d in (1, 2, 3):
+        c1(zpeer(d)).wait_send()
+        c2(beside(d)).wait_send()
+        f1(beside(d)).wait_send()
+        f2(zpeer(d)).wait_send()
     each(nv, vpeer, lambda j: y_copy(j).wait_send())
     each(plane, ppeer, lambda j: v_copy(j).wait_send())
 
     for t in range(TILES):
-        others(lambda q: q_from(t, q).wait_recv())
-        brv[t, myq] = jnp.zeros((48, width), BF16)
-        score, robust, model = fin[t, 0:16, :], fin[t, 16:32, :], fin[t, 32:48, :]
-        for q in range(ns // 2):
-            score = score + brv[t, q, 0:16, :].astype(F32)
-            robust = robust + brv[t, q, 16:32, :].astype(F32)
-            model = model + brv[t, q, 32:48, :].astype(F32)
-        cols = slice(t * width, (t + 1) * width)
-        tot_ref[0:16, cols] = score
-        tot_ref[16:32, cols] = robust
-        tot_ref[32:48, cols] = model
-
-    @pl.loop(0, TILES)
-    def _(t):
+        total = fin[t]
+        if t % 2 == 0:
+            x2(t).wait_recv()
+            total = total + lrv[t, 0].astype(F32)
+        else:
+            for d in (1, 3, 2):
+                z2_from(t, zpeer(d)).wait_recv()
+                total = total + lrv[t, zpeer(d)].astype(F32)
+        tot_ref[:, t * width : (t + 1) * width] = total
+
+    for t in range(TILES):
         a_copy(t).wait_send()
-        others(lambda q: q_copy(t, q).wait_send())
+        if t % 2 == 0:
+            x2(t).wait_send()
+            for d in (1, 2, 3):
+                z1(t, zpeer(d)).wait_send()
+        else:
+            x1(t).wait_send()
+            for d in (1, 2, 3):
+                z2(t, zpeer(d)).wait_send()
 
 
 def per_device(ns, nv, genotype, covariates, outcome, cohort, measured):
@@ -677,6 +795,8 @@
         vm((nz, 72, 128), F32),
         vm((ns, 64, 128), F32),
         vm((ns, 64, 128), F32),
+        vm((4, 64, 128), F32),
+        vm((4, 64, 128), F32),
         vm((64, 128), F32),
         vm((nz, 64, 128), F32),
         vm((64, 128), F32),
@@ -693,11 +813,14 @@
         vm((TILES, ns // 2, 64, width), BF16),
         vm((TILES, ns // 2, 48, width), BF16),
         vm((TILES, ns // 2, 48, width), BF16),
+        vm((TILES, 4, 48, width), F32),
+        vm((TILES, 4, 48, width), BF16),
+        vm((TILES, 4, 48, width), BF16),
         vm((TILES, 48, width), F32),
         dma,
     ]
     scratch += [dma((ns,))] * 4 + [dma((nz,))] * 6 + [dma((4,))] * 6 + [dma((nv,))] * 2
-    scratch += [dma((4 * nv,))] * 2 + [dma((TILES,))] * 2 + [dma((TILES, ns // 2))] * 2
+    scratch += [dma((4 * nv,))] * 2 + [dma((TILES,))] * 2 + [dma((TILES, ns // 2))] * 4
     scratch.append(pltpu.SemaphoreType.REGULAR)
     inside = pl.BlockSpec(memory_space=pltpu.VMEM)
     totals = pl.pallas_call(

time: 118 us -> 113 us (0.958)
  Pallas kernels: 115 us -> 110 us
    pallas_call x1, Pallas kernels: 115 us -> 110 us  [per_device(): pl.pallas_call(functools.partial(kernel, ns, nv), out_shape=jax.ShapeDtyp...]
where the time goes in v4:
time: 113 us
  Pallas kernels  110 us (97%)
  other arithmetic  1.77 us (2%)
    pallas_call x1, Pallas kernels, per_device(): pl.pallas_call(functools.partial(kernel, ns, nv), out_shape=jax.ShapeDtyp...  110 us

profile of v4, /device:TPU:0, one launch (start us, length us, event | category | flops | bytes accessed | tf_op | source)
XLA Modules:
  0.0 112.8 jit_solution(12329777115411259364)
XLA Ops:
  0.6 110.4 %score_tests.1 = f32[48,2048]{1,0:T(8,128)} custom-call(bf16[2048,2048]{1,0:T(8,128)(2,1)} %g_hbm.1, f32[64,2048]{1,0:T(8,128)} %bitcast.4, f32[32,2048]{1,0:T(8,128)} %bitcast.5, s32[1,2048]{1,0:T(1,128)} %bitcast.6, s32[16,32]{1,0:T(8,128)} %bitcast.7), custom_call_target="tpu_custom_call" | custom-call | tf_op jit(solution)/shard_map/score_tests/pallas_call | solution.py:826
  111.0 1.8 %rsqrt_multiply_fusion = (f32[16,2048]{1,0:T(8,128)}, f32[16,2048]{1,0:T(8,128)}) fusion(f32[48,2048]{1,0:T(8,128)} %score_tests.1), kind=kLoop, calls=%fused_computation | loop fusion | flops 131072 | bytes 655360 | tf_op jit(solution)/shard_map/mul | solution.py:838

commit v5 on v4

--- a/solution.py
+++ b/solution.py
@@ -37,6 +37,17 @@
 
 def exact_t(a, b):
     return lax.dot_general(a, b, (((1,), (1,)), ((), ())), preferred_element_type=F32)
+
+
+def linear(beta, table):
+    n = beta.shape[0]
+    hi = beta.astype(BF16).astype(F32)
+    rest = beta - hi
+    mid = rest.astype(BF16).astype(F32)
+    rows = jnp.concatenate([hi, mid, rest - mid, jnp.zeros_like(beta)], axis=0)
+    rows = jnp.concatenate([rows, rows], axis=1).astype(BF16)
+    out = dot(rows, table)
+    return out[0:n] + out[n : 2 * n] + out[2 * n : 3 * n]
 
 
 def product(x, y):
@@ -359,15 +370,7 @@
     each(4, lambda i: block_at(i), lambda j: p_copy(j).start())
 
     def products():
-        beta = bet[:, 0:64]
-        b_hi = beta.astype(BF16).astype(F32)
-        rest = beta - b_hi
-        b_mid = rest.astype(BF16).astype(F32)
-        none = jnp.zeros_like(beta)
-        rows = jnp.concatenate([b_hi, b_mid, rest - b_mid, none], axis=0)
-        rows = jnp.concatenate([rows, rows], axis=1).astype(BF16)
-        eta = dot(rows, xhl[...])
-        eta = eta[0:8] + eta[8:16] + eta[16:24]
+        eta = linear(bet[:, 0:64], xhl[...])
         fitted = 1.0 / (1.0 + jnp.exp(-eta))
         coded = y4[...]
         seen = coded >= 0.0
@@ -478,8 +481,6 @@
             b_from(zpeer(d)).wait_recv()
         rows = br[:, 0, :]
         bet[...] = jnp.concatenate([rows, pltpu.roll(rows, 64, 1)], axis=0)
-        for d in (1, 2, 3):
-            h_copy(zpeer(d)).wait_send()
 
     gcopy.wait()
     crosses()
@@ -493,11 +494,11 @@
             told, inc=1, device_id=(4 * z + lax.rem(sub + d, 4), v), device_id_type=mesh_id
         )
     x_across(1).start()
-    x_beside(1).start()
     upright()
     p_from(block_at(2)).wait_recv()
     p_from(block_at(3)).wait_recv()
     x_from(0, 3).wait_recv()
+    x_beside(1).start()
     hacc[...] += products0(1 - xh)
     send_sums()
     x_from(1, 2).wait_recv()
@@ -520,6 +521,8 @@
     @pl.loop(1, ITERS)
     def _(it):
         products()
+        for d in (1, 2, 3):
+            h_copy(zpeer(d)).wait_send()
         send_sums()
 
         @pl.when(it == 1)
@@ -580,6 +583,8 @@
 
         collect()
 
+    for d in (1, 2, 3):
+        h_copy(zpeer(d)).wait_send()
     ball[place] = bet[...]
     each(plane, ppeer, lambda j: v_copy(j).start())
     yall[v] = ybuf[...]
@@ -604,7 +609,7 @@
                 v_from(4 * u + k).wait_recv()
 
         rows = ball[pl.ds(u * 4, 4)].reshape(32, 128)
-        eta = exact(rows[:, 0:64], xt_ref[...])
+        eta = linear(rows[:, 0:64], xhl[:, own])
         fitted = 1.0 / (1.0 + jnp.exp(-eta))
         coded = yall[u]
         seen = coded >= 0.0

time: 113 us -> 113 us (level)
  no operation moved by 1% of the time
where the time goes in v5:
time: 113 us
  Pallas kernels  110 us (97%)
  other arithmetic  1.77 us (2%)
    pallas_call x1, Pallas kernels, per_device(): pl.pallas_call(functools.partial(kernel, ns, nv), out_shape=jax.ShapeDtyp...  110 us

profile of v5, /device:TPU:0, one launch (start us, length us, event | category | flops | bytes accessed | tf_op | source)
XLA Modules:
  0.0 112.7 jit_solution(13519062477533138049)
XLA Ops:
  0.6 110.3 %score_tests.1 = f32[48,2048]{1,0:T(8,128)} custom-call(bf16[2048,2048]{1,0:T(8,128)(2,1)} %g_hbm.1, f32[64,2048]{1,0:T(8,128)} %bitcast.4, f32[32,2048]{1,0:T(8,128)} %bitcast.5, s32[1,2048]{1,0:T(1,128)} %bitcast.6, s32[16,32]{1,0:T(8,128)} %bitcast.7), custom_call_target="tpu_custom_call" | custom-call | tf_op jit(solution)/shard_map/score_tests/pallas_call | solution.py:831
  111.0 1.8 %rsqrt_multiply_fusion = (f32[16,2048]{1,0:T(8,128)}, f32[16,2048]{1,0:T(8,128)}) fusion(f32[48,2048]{1,0:T(8,128)} %score_tests.1), kind=kLoop, calls=%fused_computation | loop fusion | flops 131072 | bytes 655360 | tf_op jit(solution)/shard_map/mul | solution.py:843
